TPU v7x, 512 devices: a whole 4x4x16 slice. The times are simulated.
512 devices in a mesh: terms: 8 (over x, core), sectors: 64 (over z, y).
Axes of the slice: x: 4, y: 4, z: 16, core: 2. Of those that a mesh axis runs over, the one named last changes fastest.
Arguments:
- wave: float32 [512, 64, 512], P('sectors'), may hold values from -45 to 45
- left_env: float32 [8, 512, 4096], P('terms', 'sectors'), may hold values from -3 to 3
- right_env: float32 [8, 512, 4096], P('terms', 'sectors'), may hold values from -4 to 4
- pair_target: int32 [512, 8], replicated, may hold values from 0 to 511, as said below
- block_dims: int32 [512], replicated, may hold values from 32 to 64
Outputs:
- image_two: float32 [512, 64, 512], P('sectors')
- projected: float32 [2, 2], replicated
Inputs may be any that keep to these rules, and one draw needn't show every extreme that they name: `pair_target`: every right sector is named exactly 8 times. Counting sectors in runs of 8 (a run to an index of sectors), the blocks of one run of left sectors name exactly 1 right sectors of every run.
All inputs are finite; a program needn't handle non-finite values.
Results may differ from a plain program's by a relative error of at most 0.0003.
Values sent between devices are 32-bit elements; how exact they have to be, the bound alone decides.
A program may use at most 64 MiB of HBM per device.

v0:
```python
import jax
import jax.numpy as jnp
from jax import lax
from jax.sharding import PartitionSpec as P


def slot_table(hit_table, per_peer):
    rank_run = jnp.cumsum(hit_table.astype(jnp.int32), axis=1) - 1
    wanted = jnp.arange(per_peer, dtype=jnp.int32)[None, :, None]
    chosen = hit_table[:, None, :] & (rank_run[:, None, :] == wanted)
    positions = jnp.arange(hit_table.shape[1], dtype=jnp.int32)
    return jnp.sum(jnp.where(chosen, positions[None, None, :], 0), axis=2)


def per_device(wave, left_env, right_env, pair_target, block_dims):
    dev_count = lax.axis_size("sectors")
    my_index = lax.axis_index("sectors")
    term_count = lax.axis_size("terms")
    term_index = lax.axis_index("terms")
    sec_dev = wave.shape[0]
    block_size = wave.shape[1]
    pair_count = wave.shape[2] // block_size
    groups = left_env.shape[0]
    blocks = sec_dev * pair_count
    per_peer = blocks // dev_count
    block_area = block_size * block_size
    block_ids = jnp.arange(blocks, dtype=jnp.int32)
    span = sec_dev // term_count
    wave_blocks = wave.reshape(sec_dev, block_size, pair_count, block_size).transpose(0, 2, 1, 3)
    left_blocks = left_env.reshape(groups, sec_dev, block_size, block_size)
    right_blocks = right_env.reshape(groups, sec_dev, block_size, block_size)
    my_pairs = lax.dynamic_slice_in_dim(pair_target, my_index * sec_dev, sec_dev, 0).reshape(blocks)
    peer_ids = jnp.arange(dev_count, dtype=jnp.int32)
    send_hit = (my_pairs // sec_dev)[None, :] == peer_ids[:, None]
    send_flat = slot_table(send_hit, per_peer).reshape(blocks)
    inverse = jnp.sum(
        jnp.where(send_flat[None, :] == block_ids[:, None], block_ids[None, :], 0), axis=1
    )
    everyone = pair_target.reshape(dev_count, blocks)
    recv_hit = everyone // sec_dev == my_index
    recv_idx = slot_table(recv_hit, per_peer)
    recv_pair = jnp.take_along_axis(everyone, recv_idx, axis=1)
    recv_sector = (recv_pair % sec_dev).reshape(blocks)
    left_dims = lax.dynamic_slice_in_dim(block_dims, my_index * sec_dev, sec_dev, 0)
    right_dims = jnp.take(block_dims, my_pairs, axis=0).reshape(sec_dev, pair_count)
    positions = jnp.arange(block_size, dtype=jnp.int32)
    rows_ok = positions[None, None, :, None] < left_dims[:, None, None, None]
    cols_ok = positions[None, None, None, :] < right_dims[:, :, None, None]
    valid_mask = (rows_ok & cols_ok).astype(jnp.float32)
    right_slots = jnp.take(right_blocks, recv_sector, axis=1)

    def left_apply(vector):
        moved = jnp.einsum(
            "tsab,sjbc->tsjac",
            left_blocks,
            vector,
            precision=lax.Precision.HIGHEST,
            preferred_element_type=jnp.float32,
        )
        return moved.reshape(groups, blocks, block_size, block_size)

    def term_total(partial_value, back_fn):
        return back_fn(lax.psum(partial_value, "terms"))

    def own_slice(array):
        return lax.dynamic_slice_in_dim(array, term_index * span, span, 0)

    def return_blocks(summed):
        row_count = summed.shape[1]
        arranged = summed.reshape(dev_count, per_peer, row_count * block_size)
        arrived = lax.all_to_all(arranged, "sectors", split_axis=0, concat_axis=0, tiled=True)
        return jnp.take(arrived.reshape(blocks, row_count, block_size), inverse, axis=0)

    def apply_ham(vector):
        buffer = jnp.take(left_apply(vector), send_flat, axis=1)
        buffer = buffer.reshape(groups, dev_count, per_peer, block_area)
        arrived = lax.all_to_all(buffer, "sectors", split_axis=1, concat_axis=1, tiled=True)
        arrived = arrived.reshape(groups, blocks, block_size, block_size)
        partial_value = jnp.einsum(
            "tkac,tkbc->kab",
            arrived,
            right_slots,
            precision=lax.Precision.HIGHEST,
            preferred_element_type=jnp.float32,
        )
        summed = term_total(partial_value, return_blocks)
        return summed.reshape(sec_dev, pair_count, block_size, block_size) * valid_mask

    def inner(first, second):
        return jnp.sum(own_slice(first) * own_slice(second))

    cell_total = float(dev_count * sec_dev * pair_count * block_size * block_size)
    first_vec = wave_blocks * valid_mask
    image_one = apply_ham(first_vec)
    norm_first, cross_dot = lax.psum(
        (inner(first_vec, first_vec), inner(first_vec, image_one)), ("terms", "sectors")
    )
    energy = cross_dot / norm_first
    residual = image_one - energy * first_vec
    squared = lax.psum(inner(residual, residual), ("terms", "sectors"))
    direction = residual / jnp.sqrt(squared / cell_total + 1e-06)
    image_two = apply_ham(direction)
    first_two, dir_one, dir_two = lax.psum(
        (inner(first_vec, image_two), inner(direction, image_one), inner(direction, image_two)),
        ("terms", "sectors"),
    )
    projected = (
        jnp.stack([jnp.stack([cross_dot, first_two]), jnp.stack([dir_one, dir_two])]) / cell_total
    )
    image_flat = image_two.transpose(0, 2, 1, 3).reshape(
        sec_dev, block_size, pair_count * block_size
    )
    return (image_flat, projected)


def solution(mesh):
    in_specs = (
        P("sectors", None, None),
        P("terms", "sectors", None),
        P("terms", "sectors", None),
        P(),
        P(),
    )
    out_specs = (P("sectors", None, None), P())
    return jax.shard_map(
        per_device, mesh=mesh, in_specs=in_specs, out_specs=out_specs, check_vma=False
    )
```

profile of v0, /device:TPU:1, one launch (start us, length us, event | category | flops | bytes accessed | tf_op | source)
XLA Modules:
  0.0 845.4 jit_solution(7232888239103567559)
XLA Ops:
  14.1 3.2 fusion.10
  25.4 19.5 %all-to-all-start = ((f32[1,64,1,4096]{3,2,0,1:T(1,128)}), f32[1,64,1,4096]{3,2,0,1:T(1,128)}, u32[]{:S(2)}, u32[]{:S(2)}) async-start(f32[1,64,1,4096]{3,2,0,1:T(1,128)} %reshape.611), calls=%async_computation | async-start | bytes 2097152 | tf_op jit(solution)/shard_map/all_to_all | solution.py:77
  46.4 49.7 %all-to-all-done = f32[1,64,1,4096]{3,2,0,1:T(1,128)} async-done(((f32[1,64,1,4096]{3,2,0,1:T(1,128)}), f32[1,64,1,4096]{3,2,0,1:T(1,128)}, u32[]{:S(2)}, u32[]{:S(2)}) %all-to-all-start) | async-done | bytes 1048608 | tf_op jit(solution)/shard_map/all_to_all | solution.py:77
  96.2 3.7 reduce.2
  102.1 6.5 fusion.2
  108.6 3.4 reshape.612
  112.0 72.0 %all-reduce.5.cloned.1.call-done = f32[64,1,4096]{2,1,0:T(1,128)} async-done(((f32[64,1,4096]{2,1,0:T(1,128)}), f32[64,1,4096]{2,1,0:T(1,128)}) %all-reduce.5.cloned.1.call-update) | async-done | bytes 1048592 | tf_op jit(solution)/shard_map/psum | solution.py:63
  184.0 15.2 %all-to-all-start.1 = ((f32[64,1,4096]{2,1,0:T(1,128)}), f32[64,1,4096]{2,1,0:T(1,128)}, u32[]{:S(2)}, u32[]{:S(2)}) async-start(f32[64,1,4096]{2,1,0:T(1,128)} %all-reduce.5.cloned.1.call-done), calls=%async_computation.1 | async-start | bytes 2097152 | tf_op jit(solution)/shard_map/all_to_all | solution.py:71
  199.5 48.9 %all-to-all-done.1 = f32[64,1,4096]{2,1,0:T(1,128)} async-done(((f32[64,1,4096]{2,1,0:T(1,128)}), f32[64,1,4096]{2,1,0:T(1,128)}, u32[]{:S(2)}, u32[]{:S(2)}) %all-to-all-start.1) | async-done | bytes 1048608 | tf_op jit(solution)/shard_map/all_to_all | solution.py:71
  248.3 3.7 reduce.3
  254.2 3.7 gather_fusion.4
  257.9 3.2 broadcast_select_fusion.1
  268.8 107.9 %all-reduce.1 = (f32[]{:T(128)}, f32[]{:T(128)}) all-reduce(f32[]{:T(128)} %get-tuple-element.8, f32[]{:T(128)} %get-tuple-element.7), channel_id=1, replica_groups=mesh['terms'=8,'sectors'=64] {'terms','sectors'}, use_global_device_ids=true, to_apply=%region_7.10 | all-reduce | flops 2 | bytes 16 | tf_op jit(solution)/shard_map/psum | solution.py:95
  382.6 99.5 %psum.59 = f32[]{:T(128)} all-reduce(f32[]{:T(128)} %multiply_reduce_fusion.3), channel_id=1, replica_groups=mesh['terms'=8,'sectors'=64] {'terms','sectors'}, use_global_device_ids=true, to_apply=%region_11.14 | all-reduce | flops 1 | bytes 8 | tf_op jit(solution)/shard_map/psum | solution.py:100
  484.6 3.3 fusion.8
  490.9 3.7 gather_fusion.5
  494.5 3.2 bitcast_select_fusion
  500.4 59.3 %all_to_all.20 = f32[1,64,1,4096]{3,2,0,1:T(1,128)} all-to-all(f32[1,64,1,4096]{3,2,0,1:T(1,128)S(1)} %reshape.613), channel_id=1, replica_groups=mesh['terms'=8,'sectors'=64] {'sectors'}, dimensions={1} | all-to-all | bytes 2097152 | tf_op jit(solution)/shard_map/all_to_all | solution.py:77
  559.7 3.7 reduce.4
  565.6 6.6 fusion
  572.2 3.4 reshape.614
  575.7 70.0 %all-reduce.7.cloned.1.call-done = f32[64,1,4096]{2,1,0:T(1,128)} async-done(((f32[64,1,4096]{2,1,0:T(1,128)}), f32[64,1,4096]{2,1,0:T(1,128)}) %all-reduce.7.cloned.1.call-update) | async-done | bytes 1048592 | tf_op jit(solution)/shard_map/psum | solution.py:63
  645.6 64.4 %all_to_all.21 = f32[64,1,4096]{2,1,0:T(1,128)S(1)} all-to-all(f32[64,1,4096]{2,1,0:T(1,128)} %all-reduce.7.cloned.1.call-done), channel_id=1, replica_groups=mesh['terms'=8,'sectors'=64] {'sectors'}, dimensions={0} | all-to-all | bytes 2097152 | tf_op jit(solution)/shard_map/all_to_all | solution.py:71
  727.0 108.0 %all-reduce = (f32[1]{0:T(128)}, f32[1]{0:T(128)}, f32[1]{0:T(128)}) all-reduce(f32[1]{0:T(128)} %bitcast.28, f32[1]{0:T(128)} %bitcast.27, f32[1]{0:T(128)} %bitcast.25), channel_id=1, replica_groups=mesh['terms'=8,'sectors'=64] {'terms','sectors'}, use_global_device_ids=true, to_apply=%region_18.21 | all-reduce | flops 3 | bytes 24 | tf_op jit(solution)/shard_map/psum | solution.py:103
  (87 shorter events, 62.8 us)
Async XLA Ops:
  7.2 3.9 copy-start
  7.2 4.9 copy-start.7
  7.2 5.0 copy-start.6
  12.8 1.3 copy-start.1
  14.1 3.2 copy-start.2
  23.1 22.4 %copy-start.8 = (f32[1,8,4096]{2,1,0:T(8,128)S(1)}, f32[1,8,4096]{2,1,0:T(8,128)}, u32[]{:S(2)}) copy-start(f32[1,8,4096]{2,1,0:T(8,128)} %param.11) | copy-start | bytes 393220
  25.4 70.8 %all-to-all-start = ((f32[1,64,1,4096]{3,2,0,1:T(1,128)}), f32[1,64,1,4096]{3,2,0,1:T(1,128)}, u32[]{:S(2)}, u32[]{:S(2)}) async-start(f32[1,64,1,4096]{3,2,0,1:T(1,128)} %reshape.611), calls=%async_computation | async-start | bytes 2097152 | tf_op jit(solution)/shard_map/all_to_all | solution.py:77
  44.9 139.1 %all-reduce.5.cloned.1.call-start = ((), (), s32[]{:S(2)}) async-start(), calls=%async_computation.4 | async-start | bytes 2097152 | tf_op jit(solution)/shard_map/psum | solution.py:63
  184.0 64.3 %all-to-all-start.1 = ((f32[64,1,4096]{2,1,0:T(1,128)}), f32[64,1,4096]{2,1,0:T(1,128)}, u32[]{:S(2)}, u32[]{:S(2)}) async-start(f32[64,1,4096]{2,1,0:T(1,128)} %all-reduce.5.cloned.1.call-done), calls=%async_computation.1 | async-start | bytes 2097152 | tf_op jit(solution)/shard_map/all_to_all | solution.py:71
  199.2 446.4 %all-reduce.7.cloned.1.call-start = ((), (), s32[]{:S(2)}) async-start(), calls=%async_computation.5 | async-start | bytes 2097152 | tf_op jit(solution)/shard_map/psum | solution.py:63
  265.9 1.3 copy-start.5
  380.6 1.3 copy-start.4
  484.6 3.3 copy-start.3
Sparse Core Ops, SparseCore 0:
  112.1 71.8 all-reduce.4
  575.8 69.7 all-reduce.6
where the time goes:
time: 852 us; the launch traced here: 845 us
  blocking collectives  439 us (52%)
  waiting for transfers between devices  241 us (28%)
  local copies, waits for them, and re-layouts  52.8 us (6%)
  other arithmetic  40.9 us (5%)
  starting transfers between devices  35.5 us (4%)
  matrix products  19.6 us (2%)
  between operations  16.7 us (2%)
    psum x2, waiting for transfers between devices, term_total(): return back_fn(lax.psum(partial_value, 'terms'))  142 us
    psum x1, blocking collectives, per_device(): lax.psum((inner(first_vec, image_two), inner(direction, image_one), inner...  108 us
    psum x1, blocking collectives, per_device(): lax.psum((inner(first_vec, first_vec), inner(first_vec, image_one)), ('te...  108 us
    psum x1, blocking collectives, per_device(): squared = lax.psum(inner(residual, residual), ('terms', 'sectors'))  99.5 us
    all_to_all x1, blocking collectives, return_blocks(): lax.all_to_all(arranged, 'sectors', split_axis=0, concat_axis=0, tiled=True)  64.4 us
    all_to_all x1, blocking collectives, apply_ham(): lax.all_to_all(buffer, 'sectors', split_axis=1, concat_axis=1, tiled=True)  59.3 us
    all_to_all x1, waiting for transfers between devices, apply_ham(): lax.all_to_all(buffer, 'sectors', split_axis=1, concat_axis=1, tiled=True)  49.7 us
    all_to_all x1, waiting for transfers between devices, return_blocks(): lax.all_to_all(arranged, 'sectors', split_axis=0, concat_axis=0, tiled=True)  48.9 us
  transfers between devices with their start and end apart: 4, of which 4 were waited for; matrix products, arithmetic and copies ran while one was open for 0% of the time, Pallas kernels for 0%

commit v1 on v0

v1 whole, which is shorter than its diff:
```python
import functools

import jax
import jax.numpy as jnp
from jax import lax
from jax.experimental import pallas as pl
from jax.experimental.pallas import tpu as pltpu
from jax.sharding import PartitionSpec as P

MESH = pl.DeviceIdType.MESH
DB = 64
LANES = 128
HALF = DB // 2
WIDE_Y = 4
TINY = 1e-30
NAMES = ("n", "c", "rr", "rf", "fg", "ri", "rg", "e")


def lane_low(rows):
    return lax.broadcasted_iota(jnp.int32, (rows, LANES), 1) < DB


def swap(x):
    return pltpu.roll(x, DB, 1)


def split(x):
    high = x.astype(jnp.bfloat16)
    low = (x - high.astype(jnp.float32)).astype(jnp.bfloat16)
    return high, low


def total(x):
    return jnp.sum(jnp.sum(x, axis=0, keepdims=True), axis=1, keepdims=True)


def recenter(stat, center):
    shift = stat["e"] - center
    return {
        "n": stat["n"],
        "c": stat["c"],
        "rr": stat["rr"] + 2.0 * shift * stat["rf"] + shift * shift * stat["n"],
        "rf": stat["rf"] + shift * stat["n"],
        "fg": stat["fg"] + shift * stat["c"],
        "ri": stat["ri"] + shift * stat["c"],
        "rg": stat["rg"] + shift * (stat["ri"] + stat["fg"]) + shift * shift * stat["c"],
    }


def quotient(cross, norm):
    return jnp.where(norm > TINY, cross / jnp.maximum(norm, TINY), 0.0)


def merge(stat, last):
    norm = jnp.sum(stat["n"], axis=0, keepdims=True)
    cross = jnp.sum(stat["c"], axis=0, keepdims=True)
    center = cross / norm if last else quotient(cross, norm)
    moved = recenter(stat, center)
    out = {name: jnp.sum(value, axis=0, keepdims=True) for name, value in moved.items()}
    out["e"] = center
    return out


def read_rows(buf):
    rows = buf[:, 0, :]
    return {name: rows[:, k : k + 1] for k, name in enumerate(NAMES)}


def row_of(stat):
    lane = lax.broadcasted_iota(jnp.int32, (1, LANES), 1)
    row = jnp.zeros((1, LANES), jnp.float32)
    for k, name in enumerate(NAMES):
        row = jnp.where(lane == k, stat[name], row)
    return row


def repack(src, dst):
    low = lane_low(src.shape[0])
    for u in range(HALF // 2):
        first = src[:, LANES * u : LANES * (u + 1)]
        second = src[:, LANES * (u + HALF // 2) : LANES * (u + HALF // 2 + 1)]
        dst[:, 2 * u, :] = jnp.where(low, first, swap(second))
        dst[:, 2 * u + 1, :] = jnp.where(low, swap(first), second)


def kernel(
    geo,
    cells,
    tab,
    dims,
    wave_hbm,
    left_ref,
    right_ref,
    out_ref,
    proj_ref,
    wave,
    zbuf,
    stage,
    rrecv,
    lall,
    lbf,
    wcat,
    rcat,
    ibuf,
    gbuf,
    stat_ref,
    red_a,
    red_b,
    fbuf,
    wave_sem,
    z_send,
    z_recv,
    p_send,
    p_recv,
    l_send,
    l_recv,
    a_send,
    a_recv,
    b_send,
    b_recv,
    f_send,
    f_recv,
):
    wide_x, wide_y, wide_z = geo
    terms = 2 * wide_x
    nblk = wide_z // 2
    half_z = wide_z // 2
    sec = left_ref.shape[0]
    chunks = z_send.shape[1]
    csec = sec // chunks
    plane = terms * wide_y

    my_t = lax.axis_index("terms")
    my_s = lax.axis_index("sectors")
    my_x = my_t // 2
    my_c = my_t % 2
    my_z = my_s // wide_y
    my_y = my_s % wide_y

    def dev(t, z, y):
        return {"terms": t, "sectors": z * wide_y + y}

    def plane_peer(i):
        other = lax.rem(my_t * wide_y + my_y + i, plane)
        return dev(other // wide_y, my_z, other % wide_y)

    def z_peer(i):
        return dev(my_t, lax.rem(my_z + i, wide_z), my_y)

    barrier = pltpu.get_barrier_semaphore()

    def greet_plane(i, carry):
        pl.semaphore_signal(barrier, inc=1, device_id=plane_peer(i), device_id_type=MESH)
        return carry

    def greet_z(i, carry):
        pl.semaphore_signal(barrier, inc=1, device_id=z_peer(i), device_id_type=MESH)
        return carry

    lax.fori_loop(1, wide_z, greet_z, 0)
    lax.fori_loop(1, plane, greet_plane, 0)
    wave_copy = pltpu.make_async_copy(wave_hbm, wave, wave_sem)
    wave_copy.start()
    repack(right_ref, zbuf.at[0])
    repack(left_ref, lall.at[my_t])
    pl.semaphore_wait(barrier, plane - 1 + wide_z - 1)

    def z_copy(src, dst, k, peer):
        part = pl.ds(k * csec, csec)
        return pltpu.make_async_remote_copy(
            src_ref=zbuf.at[src, part],
            dst_ref=zbuf.at[dst, part],
            send_sem=z_send.at[dst, k],
            recv_sem=z_recv.at[dst, k],
            device_id=peer,
            device_id_type=MESH,
        )

    up, down = z_peer(1), z_peer(wide_z - 1)

    def forward_up(d, k):
        z_copy(d, d + 1, k, up).start()

    def forward_down(d, k):
        z_copy(lax.rem(wide_z - d, wide_z), wide_z - 1 - d, k, down).start()

    sibling = dev(my_t + 1 - 2 * my_c, my_z, my_y)

    def l_copy(t, peer, k):
        return pltpu.make_async_remote_copy(
            src_ref=lall.at[t],
            dst_ref=lall.at[t],
            send_sem=l_send.at[k],
            recv_sem=l_recv.at[t],
            device_id=peer,
            device_id_type=MESH,
        )

    def x_term(i):
        return lax.rem(my_x + i, wide_x) * 2 + my_c

    for k in range(chunks):
        forward_up(0, k)
        forward_down(0, k)
    for i in range(1, wide_x):
        l_copy(my_t, dev(x_term(i), my_z, my_y), i - 1).start()
    l_copy(my_t, sibling, wide_x - 1).start()

    def owner(o, yp):
        t = 2 * lax.rem(my_y + yp + o, wide_x) + o // half_z
        return t, jnp.logical_and(t == my_t, yp == my_y)

    def remote_piece(o, yp):
        t, _ = owner(o, yp)
        return pltpu.make_async_remote_copy(
            src_ref=stage.at[o, yp],
            dst_ref=rrecv.at[lax.rem(o, half_z), my_t],
            send_sem=p_send.at[o, yp],
            recv_sem=p_recv.at[lax.rem(o, half_z)],
            device_id=dev(t, my_z, yp),
            device_id_type=MESH,
        )

    def local_piece(o, yp):
        b = lax.rem(o, half_z)
        return pltpu.make_async_copy(stage.at[o, yp], rrecv.at[b, my_t], p_recv.at[b])

    def hand_out(o):
        def one(yp, carry):
            wanted = jnp.full((HALF, LANES), tab[o * wide_y + yp], jnp.int32)
            got = zbuf[o, 0]
            for k in range(1, sec):
                got = jnp.where(wanted == k, zbuf[o, k], got)
            stage[o, yp] = got
            _, mine = owner(o, yp)

            @pl.when(mine)
            def _():
                local_piece(o, yp).start()

            @pl.when(jnp.logical_not(mine))
            def _():
                remote_piece(o, yp).start()

            return carry

        lax.fori_loop(0, wide_y, one, 0)

    def arrive(o, k):
        z_copy(o, o, k, up).wait_recv()

    def z_step(d):
        def part(k, carry):
            arrive(d, k)
            forward_up(d, k)
            arrive(wide_z - d, k)
            forward_down(d, k)
            return carry

        lax.fori_loop(0, chunks, part, 0)
        hand_out(d)
        hand_out(wide_z - d)

    def z_step_before_last(d):
        for k in range(chunks):
            arrive(d, k)
            if k < chunks // 2:
                forward_up(d, k)
            arrive(wide_z - d, k)
            if k >= chunks // 2:
                forward_down(d, k)
        hand_out(d)
        hand_out(wide_z - d)

    def z_step_last(d):
        for k in range(chunks):
            arrive(d, k)
        hand_out(d)

    low64 = lane_low(DB)
    low32 = lane_low(HALF)
    slot_at = wide_z * wide_y
    sector_at = slot_at + cells
    column_at = sector_at + nblk
    odd_at = column_at + nblk
    target_at = odd_at + nblk
    pairs = cells // sec

    def apply(vec, q):
        vh, vl = split(vec)
        rhs = jnp.concatenate([vh, vh, vl, vl], axis=0)
        for u in range(terms // 2):
            lhs = lbf[q, pl.ds(u * LANES, LANES), :]
            both = jnp.dot(
                jnp.concatenate([lhs, lhs], axis=1), rhs, preferred_element_type=jnp.float32
            )
            high, low = split(jnp.where(low64, both[:DB], both[DB:]))
            wcat[:DB, u * LANES : (u + 1) * LANES] = high
            wcat[DB:, u * LANES : (u + 1) * LANES] = low
        out = lax.dot_general(
            wcat[...], rcat[...], (((1,), (1,)), ((), ())), preferred_element_type=jnp.float32
        )
        out = out[:DB] + out[DB:]
        return out + swap(out)

    def pack(x):
        return jnp.where(low32, x[:HALF], x[HALF:])

    def work(i):
        b = jnp.where(my_c == 0, i, nblk - 1 - i)
        pltpu.make_async_copy(rrecv.at[b], rrecv.at[b], p_recv.at[b]).wait()
        for u in range(terms // 2):
            first, second = rrecv[b, 2 * u], rrecv[b, 2 * u + 1]
            top = jnp.where(low32, first, swap(second))
            bottom = jnp.where(low32, swap(first), second)
            high, low = split(jnp.concatenate([top, bottom], axis=0))
            rcat[:DB, u * LANES : (u + 1) * LANES] = high
            rcat[DB:, u * LANES : (u + 1) * LANES] = low
        q = tab[sector_at + b]
        column = jnp.full((DB, LANES), tab[column_at + b], jnp.int32)
        odd = jnp.full((DB, LANES), tab[odd_at + b], jnp.int32)
        raw = wave[q, :, 0:LANES]
        for u in range(1, pairs // 2):
            raw = jnp.where(column == u, wave[q, :, u * LANES : (u + 1) * LANES], raw)
        lane = lax.broadcasted_iota(jnp.int32, (DB, LANES), 1)
        row = lax.broadcasted_iota(jnp.int32, (DB, LANES), 0)
        raw = jnp.where(lane // DB == odd, raw, swap(raw))
        used = jnp.logical_and(
            row < dims[my_s * sec + q], lax.rem(lane, DB) < dims[tab[target_at + b]]
        )
        first = jnp.where(used, raw, 0.0)
        image = jnp.where(used, apply(first, q), 0.0)
        norm = 0.5 * total(first * first)
        cross = 0.5 * total(first * image)
        energy = quotient(cross, norm)
        rest = image - energy * first
        second = jnp.where(used, apply(rest, q), 0.0)
        ibuf[b] = pack(image)
        gbuf[b] = pack(second)
        values = (
            norm,
            cross,
            0.5 * total(rest * rest),
            0.5 * total(rest * first),
            0.5 * total(first * second),
            0.5 * total(rest * image),
            0.5 * total(rest * second),
            energy,
        )
        sub = lax.broadcasted_iota(jnp.int32, (8, LANES), 0)
        tile = jnp.zeros((8, LANES), jnp.float32)
        for k, value in enumerate(values):
            tile = jnp.where(sub == k, value, tile)
        stat_ref[b] = tile

    def unpack_left():
        def one(t, carry):
            for q in range(sec):
                x = lall[t, q]
                high, low = split(x)
                high, low = high.astype(jnp.float32), low.astype(jnp.float32)
                top = jnp.where(low32, high, swap(low))
                bottom = jnp.where(low32, swap(high), low)
                both = jnp.concatenate([top, bottom], axis=0).astype(jnp.bfloat16)
                lbf[q, pl.ds(pl.multiple_of(t * DB, DB), DB), :] = both
            return carry

        lax.fori_loop(0, terms, one, 0)

    early = min(3, half_z - 1)
    hand_out(0)
    for i in range(1, wide_x):
        t = x_term(i)
        l_copy(t, sibling, 0).wait_recv()
        l_copy(t, sibling, wide_x - 1 + i).start()
    lax.fori_loop(1, early, lambda d, c: (z_step(d), c)[1], 0)
    for i in range(wide_x):
        l_copy(lax.rem(my_x + i, wide_x) * 2 + 1 - my_c, sibling, 0).wait_recv()
    unpack_left()
    wave_copy.wait()

    def mixed(d, carry):
        z_step(d)
        work(d - early)
        return carry

    lax.fori_loop(early, half_z - 1, mixed, 0)
    z_step_before_last(half_z - 1)
    work(half_z - 1 - early)
    z_step_last(half_z)

    def rest_of_work(i, carry):
        work(i)
        return carry

    lax.fori_loop(half_z - early, nblk, rest_of_work, 0)

    stat = {name: stat_ref[:, k, :] for k, name in enumerate(NAMES)}
    mine = my_t * wide_y + my_y
    red_a[mine] = row_of(merge(stat, False))

    def a_copy(i):
        return pltpu.make_async_remote_copy(
            src_ref=red_a.at[mine],
            dst_ref=red_a.at[mine],
            send_sem=a_send.at[i],
            recv_sem=a_recv,
            device_id=plane_peer(i),
            device_id_type=MESH,
        )

    def b_copy(i):
        return pltpu.make_async_remote_copy(
            src_ref=red_b.at[my_z],
            dst_ref=red_b.at[my_z],
            send_sem=b_send.at[i],
            recv_sem=b_recv,
            device_id=z_peer(i),
            device_id_type=MESH,
        )

    lax.fori_loop(1, plane, lambda i, c: (a_copy(i).start(), c)[1], 0)
    pltpu.make_async_copy(
        red_a.at[pl.ds(0, plane - 1)], red_a.at[pl.ds(0, plane - 1)], a_recv
    ).wait()
    red_b[my_z] = row_of(merge(read_rows(red_a), False))
    lax.fori_loop(1, wide_z, lambda i, c: (b_copy(i).start(), c)[1], 0)
    pltpu.make_async_copy(
        red_b.at[pl.ds(0, wide_z - 1)], red_b.at[pl.ds(0, wide_z - 1)], b_recv
    ).wait()
    final = merge(read_rows(red_b), True)
    cell_total = float(plane * wide_z * nblk * DB * DB)
    squared = jnp.maximum(final["rr"], 0.0)
    scale = 1.0 / jnp.sqrt(squared / cell_total + 1e-06)
    sub2 = lax.broadcasted_iota(jnp.int32, (2, 2), 0)
    lane2 = lax.broadcasted_iota(jnp.int32, (2, 2), 1)
    proj_ref[...] = (
        jnp.where(
            sub2 == 0,
            jnp.where(lane2 == 0, final["c"], final["fg"] * scale),
            jnp.where(lane2 == 0, final["ri"] * scale, final["rg"] * scale * scale),
        )
        / cell_total
    )

    center = final["e"]
    for b in range(nblk):
        shift = stat_ref[b, 7:8, :] - center
        fbuf[my_t * nblk + b] = (gbuf[b] + shift * ibuf[b]) * scale

    def f_copy(t, peer, k):
        return pltpu.make_async_remote_copy(
            src_ref=fbuf.at[pl.ds(t * nblk, nblk)],
            dst_ref=fbuf.at[pl.ds(t * nblk, nblk)],
            send_sem=f_send.at[k],
            recv_sem=f_recv.at[t],
            device_id=peer,
            device_id_type=MESH,
        )

    for i in range(1, wide_x):
        f_copy(my_t, dev(x_term(i), my_z, my_y), i - 1).start()
    f_copy(my_t, sibling, wide_x - 1).start()
    for i in range(1, wide_x):
        t = x_term(i)
        f_copy(t, sibling, 0).wait_recv()
        f_copy(t, sibling, wide_x - 1 + i).start()
    for i in range(wide_x):
        f_copy(lax.rem(my_x + i, wide_x) * 2 + 1 - my_c, sibling, 0).wait_recv()

    def place(q, carry):
        for u in range(pairs // 2):
            first_at = tab[slot_at + q * pairs + 2 * u]
            second_at = tab[slot_at + q * pairs + 2 * u + 1]
            first = fbuf[first_at]
            second = fbuf[second_at]
            out_ref[q, 0:HALF, u * LANES : (u + 1) * LANES] = jnp.where(
                low32, first, swap(second)
            )
            out_ref[q, HALF:DB, u * LANES : (u + 1) * LANES] = jnp.where(
                low32, swap(first), second
            )
        return carry

    lax.fori_loop(0, sec, place, 0)

    def z_done(d, carry):
        for k in range(chunks):
            z_copy(0, d + 1, k, up).wait_send()
            z_copy(0, wide_z - 1 - d, k, down).wait_send()
        return carry

    lax.fori_loop(0, half_z - 1, z_done, 0)
    for k in range(chunks):
        z_copy(0, half_z, k, up).wait_send()

    def p_done(n, carry):
        o, yp = n // wide_y, lax.rem(n, wide_y)
        _, mine = owner(o, yp)

        @pl.when(jnp.logical_not(mine))
        def _():
            remote_piece(o, yp).wait_send()

        return carry

    lax.fori_loop(0, wide_z * wide_y, p_done, 0)
    for i in range(2 * wide_x - 1):
        l_copy(my_t, sibling, i).wait_send()
        f_copy(my_t, sibling, i).wait_send()
    lax.fori_loop(1, plane, lambda i, c: (a_copy(i).wait_send(), c)[1], 0)
    lax.fori_loop(1, wide_z, lambda i, c: (b_copy(i).wait_send(), c)[1], 0)


def tables(geo, sec, pairs, pair_target):
    wide_x, wide_y, wide_z = geo
    nblk = wide_z // 2
    half_z = wide_z // 2
    my_t = lax.axis_index("terms")
    my_s = lax.axis_index("sectors")
    my_z, my_y = my_s // wide_y, my_s % wide_y
    cells = sec * pairs
    plane = lax.dynamic_slice_in_dim(pair_target, my_z * wide_y * sec, wide_y * sec, 0)
    plane = plane.reshape(wide_y, cells)
    offsets = jnp.arange(wide_z, dtype=jnp.int32)
    run = jnp.remainder(my_z - offsets, wide_z) * wide_y + my_y
    hit = (plane // sec)[None, :, :] == run[:, None, None]
    wanted = jnp.sum(jnp.where(hit, (plane % sec)[None, :, :], 0), axis=2).reshape(-1)
    own = lax.dynamic_slice_in_dim(pair_target, my_s * sec, sec, 0).reshape(cells)
    own_run = own // sec
    offset = jnp.remainder(my_z - own_run // wide_y, wide_z)
    holder = 2 * ((own_run % wide_y + my_y + offset) % wide_x) + offset // half_z
    slot = holder * nblk + offset % half_z
    chosen = slot[None, :] == (my_t * nblk + jnp.arange(nblk, dtype=jnp.int32))[:, None]
    cell = jnp.sum(jnp.where(chosen, jnp.arange(cells, dtype=jnp.int32)[None, :], 0), axis=1)
    target = jnp.sum(jnp.where(chosen, own[None, :], 0), axis=1)
    column = cell % pairs
    return jnp.concatenate([wanted, slot, cell // pairs, column // 2, column % 2, target])


def per_device(wide_y, wave, left_env, right_env, pair_target, block_dims):
    terms = lax.axis_size("terms")
    devices = lax.axis_size("sectors")
    geo = (terms // 2, wide_y, devices // wide_y)
    sec = wave.shape[0]
    pairs = wave.shape[2] // DB
    cells = sec * pairs
    nblk = geo[2] // 2
    plane = terms * wide_y
    chunks = 2
    tab = tables(geo, sec, pairs, pair_target)
    f32, bf16 = jnp.float32, jnp.bfloat16
    dma = pltpu.SemaphoreType.DMA
    vmem = pl.BlockSpec(memory_space=pltpu.VMEM)
    smem = pl.BlockSpec(memory_space=pltpu.SMEM)
    return pl.pallas_call(
        functools.partial(kernel, geo, cells),
        out_shape=(
            jax.ShapeDtypeStruct(wave.shape, f32),
            jax.ShapeDtypeStruct((2, 2), f32),
        ),
        in_specs=[smem, smem, pl.BlockSpec(memory_space=pl.ANY), vmem, vmem],
        out_specs=(vmem, vmem),
        scratch_shapes=[
            pltpu.VMEM(wave.shape, f32),
            pltpu.VMEM((geo[2], sec, HALF, LANES), f32),
            pltpu.VMEM((geo[2], wide_y, HALF, LANES), f32),
            pltpu.VMEM((nblk, terms, HALF, LANES), f32),
            pltpu.VMEM((terms, sec, HALF, LANES), f32),
            pltpu.VMEM((sec, terms * DB, LANES), bf16),
            pltpu.VMEM((LANES, terms * DB), bf16),
            pltpu.VMEM((LANES, terms * DB), bf16),
            pltpu.VMEM((nblk, HALF, LANES), f32),
            pltpu.VMEM((nblk, HALF, LANES), f32),
            pltpu.VMEM((nblk, 8, LANES), f32),
            pltpu.VMEM((plane, 1, LANES), f32),
            pltpu.VMEM((geo[2], 1, LANES), f32),
            pltpu.VMEM((terms * nblk, HALF, LANES), f32),
            dma,
            dma((geo[2], chunks)),
            dma((geo[2], chunks)),
            dma((geo[2], wide_y)),
            dma((nblk,)),
            dma((2 * geo[0] - 1,)),
            dma((terms,)),
            dma((plane,)),
            dma,
            dma((geo[2],)),
            dma,
            dma((2 * geo[0] - 1,)),
            dma((terms,)),
        ],
        compiler_params=pltpu.CompilerParams(
            collective_id=0, has_side_effects=True, vmem_limit_bytes=32 * 1024 * 1024
        ),
    )(
        tab,
        block_dims,
        wave,
        left_env.reshape(sec, DB * DB),
        right_env.reshape(sec, DB * DB),
    )


def solution(mesh, wide_y=WIDE_Y):
    in_specs = (
        P("sectors", None, None),
        P("terms", "sectors", None),
        P("terms", "sectors", None),
        P(),
        P(),
    )
    out_specs = (P("sectors", None, None), P())
    return jax.shard_map(
        functools.partial(per_device, wide_y),
        mesh=mesh,
        in_specs=in_specs,
        out_specs=out_specs,
        check_vma=False,
    )
```

time: 852 us -> 90.9 us (0.11)
  blocking collectives: 439 us -> 0 us
  waiting for transfers between devices: 241 us -> 0 us
  Pallas kernels: 0 us -> 83.8 us
  local copies, waits for them, and re-layouts: 52.8 us -> 5.64 us
  other arithmetic: 40.9 us -> 0.5 us
  starting transfers between devices: 35.5 us -> 0 us
  matrix products: 19.6 us -> 0 us
  between operations: 16.7 us -> 0.73 us
    psum x3 -> x0, blocking collectives: 315 us -> none  [the longest x1 108 us: per_device(): lax.psum((inner(first_vec, image_two), inner(direction, image_one), inner...]
    psum x2 -> x0, waiting for transfers between devices: 142 us -> none  [term_total(): return back_fn(lax.psum(partial_value, 'terms'))]
    all_to_all x2 -> x0, blocking collectives: 124 us -> none  [the longest x1 64.4 us: return_blocks(): lax.all_to_all(arranged, 'sectors', split_axis=0, concat_axis=0, tiled=True)]
    all_to_all x2 -> x0, waiting for transfers between devices: 98.6 us -> none  [the longest x1 49.7 us: apply_ham(): lax.all_to_all(buffer, 'sectors', split_axis=1, concat_axis=1, tiled=True)]
    pallas_call x0 -> x1, Pallas kernels: none -> 83.8 us  [per_device(): pl.pallas_call(functools.partial(kernel, geo, cells), out_shape=(jax.Shap...]
    all_to_all x2 -> x0, starting transfers between devices: 34.7 us -> none  [the longest x1 19.5 us: apply_ham(): lax.all_to_all(buffer, 'sectors', split_axis=1, concat_axis=1, tiled=True)]
    reshape x17 -> x3, local copies, waits for them, and re-layouts: 29.5 us -> 0.26 us  [the longest x1 0.1 us: tables(): jnp.sum(jnp.where(hit, (plane % sec)[None, :, :], 0), axis=2).reshape(-1)]
    dot_general x4 -> x0, matrix products: 19.6 us -> none  [the longest x2 13.1 us: apply_ham(): jnp.einsum('tkac,tkbc->kab', arrived, right_slots, precision=lax.Precisio...]
  transfers between devices with their start and end apart: 4 -> 0, of which waited for: 4 -> 0; matrix products, arithmetic and copies ran while one was open for 0% -> 0% of each run, Pallas kernels for 0% -> 0%
where the time goes in v1:
time: 90.9 us; the launch traced here: 90.7 us
  Pallas kernels  83.8 us (92%)
  local copies, waits for them, and re-layouts  5.64 us (6%)
    pallas_call x1, Pallas kernels, per_device(): pl.pallas_call(functools.partial(kernel, geo, cells), out_shape=(jax.Shap...  83.8 us
    unnamed x12, local copies, waits for them, and re-layouts  4.91 us

profile of v1, /device:TPU:1, one launch (start us, length us, event | category | flops | bytes accessed | tf_op | source)
XLA Modules:
  0.0 90.7 jit_solution(10868546758380199452)
XLA Ops:
  0.6 0.0 copy-start
  0.6 0.0 copy-start.2
  0.7 0.6 copy-done
  1.4 0.1 constant_dynamic-slice_fusion
  1.4 0.1 copy.12
  1.5 0.1 reshape.201
  1.6 0.2 fusion.1
  1.8 0.1 constant_dynamic-slice_fusion.1
  1.9 0.1 copy.10
  2.0 0.1 reshape.199
  2.1 0.2 select_reduce_fusion
  2.3 0.1 copy.11
  2.4 0.1 reshape.200
  2.5 0.0 copy-start.4
  2.5 0.1 concatenate.3.tab
  2.6 0.0 copy-done.2
  2.6 0.6 copy-done.4
  3.2 0.0 copy-start.1
  3.2 1.2 %copy-done.1 = f32[8,64,512]{2,1,0:T(8,128)S(1)} copy-done((f32[8,64,512]{2,1,0:T(8,128)S(1)}, f32[8,64,512]{2,1,0:T(8,128)}, u32[]{:S(2)}) %copy-start.1) | copy-done | bytes 1048600
  4.4 0.0 copy-start.3
  4.4 0.9 copy-done.3
  5.3 83.8 %shard_map.68 = (f32[8,64,512]{2,1,0:T(8,128)S(1)}, f32[2,2]{1,0:T(2,128)S(1)}) custom-call(s32[160]{0:T(256)S(1)} %concatenate.3.tab, s32[512]{0:T(512)S(1)} %copy-done.4, f32[8,64,512]{2,1,0:T(8,128)S(1)} %copy-done.1, f32[8,4096]{1,0:T(8,128)S(1)} %bitcast.2, f32[8,4096]{1,0:T(8,128)S(1)} %bitcast.3), custom_call_target="tpu_custom_call" | custom-call | tf_op jit(solution)/shard_map/pallas_call | solution.py:556
  89.1 1.0 %copy.15 = f32[8,64,512]{2,1,0:T(8,128)} copy(f32[8,64,512]{2,1,0:T(8,128)S(1)} %get-tuple-element.13) | data formatting | bytes 2097152
  90.1 0.6 copy.16
  (6 shorter events, 0.1 us)
Async XLA Ops:
  0.6 0.7 copy-start
  0.6 2.0 %copy-start.2 = (f32[1,8,4096]{2,1,0:T(8,128)S(1)}, f32[1,8,4096]{2,1,0:T(8,128)}, u32[]{:S(2)}) copy-start(f32[1,8,4096]{2,1,0:T(8,128)} %param.6) | copy-start | bytes 393220
  2.5 0.7 copy-start.4
  3.2 1.2 %copy-start.1 = (f32[8,64,512]{2,1,0:T(8,128)S(1)}, f32[8,64,512]{2,1,0:T(8,128)}, u32[]{:S(2)}) copy-start(f32[8,64,512]{2,1,0:T(8,128)} %wave_hbm.1) | copy-start | bytes 3145732
  4.4 0.9 copy-start.3

commit v2 on v1

--- a/solution.py
+++ b/solution.py
@@ -12,6 +12,7 @@
 LANES = 128
 HALF = DB // 2
 WIDE_Y = 4
+STRIDE = 2
 TINY = 1e-30
 NAMES = ("n", "c", "rr", "rf", "fg", "ri", "rg", "e")
 
@@ -101,12 +102,9 @@
     lbf,
     wcat,
     rcat,
-    ibuf,
     gbuf,
-    stat_ref,
     red_a,
     red_b,
-    fbuf,
     wave_sem,
     z_send,
     z_recv,
@@ -118,8 +116,11 @@
     a_recv,
     b_send,
     b_recv,
-    f_send,
-    f_recv,
+    g_send,
+    g_pass,
+    g_recv,
+    plane_sem,
+    space_sem,
 ):
     wide_x, wide_y, wide_z = geo
     terms = 2 * wide_x
@@ -147,23 +148,27 @@
     def z_peer(i):
         return dev(my_t, lax.rem(my_z + i, wide_z), my_y)
 
+    def y_peer(i):
+        return dev(my_t, my_z, lax.rem(my_y + i, wide_y))
+
+    def term_peer(i):
+        return dev(lax.rem(my_t + i, terms), my_z, my_y)
+
     barrier = pltpu.get_barrier_semaphore()
-
-    def greet_plane(i, carry):
-        pl.semaphore_signal(barrier, inc=1, device_id=plane_peer(i), device_id_type=MESH)
-        return carry
-
-    def greet_z(i, carry):
-        pl.semaphore_signal(barrier, inc=1, device_id=z_peer(i), device_id_type=MESH)
-        return carry
-
-    lax.fori_loop(1, wide_z, greet_z, 0)
-    lax.fori_loop(1, plane, greet_plane, 0)
+    near = sorted({1, STRIDE, wide_z - STRIDE, wide_z - 1})
+
+    def tell(sem, peers):
+        for peer in peers:
+            pl.semaphore_signal(sem, inc=1, device_id=peer, device_id_type=MESH)
+
+    z_near = [z_peer(i) for i in near]
+    y_near = [y_peer(i) for i in range(1, wide_y)]
+    tell(barrier, z_near + y_near + [term_peer(i) for i in range(1, terms)])
     wave_copy = pltpu.make_async_copy(wave_hbm, wave, wave_sem)
     wave_copy.start()
     repack(right_ref, zbuf.at[0])
     repack(left_ref, lall.at[my_t])
-    pl.semaphore_wait(barrier, plane - 1 + wide_z - 1)
+    pl.semaphore_wait(barrier, len(near) + wide_y - 1 + terms - 1)
 
     def z_copy(src, dst, k, peer):
         part = pl.ds(k * csec, csec)
@@ -176,13 +181,13 @@
             device_id_type=MESH,
         )
 
-    up, down = z_peer(1), z_peer(wide_z - 1)
-
-    def forward_up(d, k):
-        z_copy(d, d + 1, k, up).start()
-
-    def forward_down(d, k):
-        z_copy(lax.rem(wide_z - d, wide_z), wide_z - 1 - d, k, down).start()
+    up, down = z_peer(STRIDE), z_peer(wide_z - STRIDE)
+
+    def forward_up(o, k):
+        z_copy(o, o + STRIDE, k, up).start()
+
+    def forward_down(o, k):
+        z_copy(o, (o + wide_z - STRIDE) % wide_z, k, down).start()
 
     sibling = dev(my_t + 1 - 2 * my_c, my_z, my_y)
 
@@ -206,76 +211,91 @@
         l_copy(my_t, dev(x_term(i), my_z, my_y), i - 1).start()
     l_copy(my_t, sibling, wide_x - 1).start()
 
-    def owner(o, yp):
-        t = 2 * lax.rem(my_y + yp + o, wide_x) + o // half_z
+    tell(plane_sem, y_near)
+    pl.semaphore_wait(plane_sem, wide_y - 1)
+    tell(space_sem, z_near)
+    pl.semaphore_wait(space_sem, len(near))
+
+    def owner(far, step, yp):
+        t = 2 * lax.rem(my_y + yp + far, wide_x) + far // half_z
+        if step != 0:
+            return t, jnp.bool_(False)
         return t, jnp.logical_and(t == my_t, yp == my_y)
 
-    def remote_piece(o, yp):
-        t, _ = owner(o, yp)
+    def remote_piece(far, step, yp):
+        t, _ = owner(far, step, yp)
         return pltpu.make_async_remote_copy(
-            src_ref=stage.at[o, yp],
-            dst_ref=rrecv.at[lax.rem(o, half_z), my_t],
-            send_sem=p_send.at[o, yp],
-            recv_sem=p_recv.at[lax.rem(o, half_z)],
-            device_id=dev(t, my_z, yp),
+            src_ref=stage.at[far, yp],
+            dst_ref=rrecv.at[far % half_z, my_t],
+            send_sem=p_send.at[far, yp],
+            recv_sem=p_recv.at[far % half_z],
+            device_id=dev(t, lax.rem(my_z + (wide_z + step), wide_z), yp),
             device_id_type=MESH,
         )
 
-    def local_piece(o, yp):
-        b = lax.rem(o, half_z)
-        return pltpu.make_async_copy(stage.at[o, yp], rrecv.at[b, my_t], p_recv.at[b])
-
-    def hand_out(o):
+    def local_piece(far, yp):
+        b = far % half_z
+        return pltpu.make_async_copy(stage.at[far, yp], rrecv.at[b, my_t], p_recv.at[b])
+
+    def hand_out(o, step, first, last):
+        far = (o + step) % wide_z
+
         def one(yp, carry):
-            wanted = jnp.full((HALF, LANES), tab[o * wide_y + yp], jnp.int32)
+            wanted = jnp.full((HALF, LANES), tab[far * wide_y + yp], jnp.int32)
             got = zbuf[o, 0]
             for k in range(1, sec):
                 got = jnp.where(wanted == k, zbuf[o, k], got)
-            stage[o, yp] = got
-            _, mine = owner(o, yp)
+            stage[far, yp] = got
+            if step != 0:
+                remote_piece(far, step, yp).start()
+                return carry
+            _, mine = owner(far, step, yp)
 
             @pl.when(mine)
             def _():
-                local_piece(o, yp).start()
+                local_piece(far, yp).start()
 
             @pl.when(jnp.logical_not(mine))
             def _():
-                remote_piece(o, yp).start()
+                remote_piece(far, step, yp).start()
 
             return carry
 
-        lax.fori_loop(0, wide_y, one, 0)
+        lax.fori_loop(first, last, one, 0)
+
+    def sent(o, step, first, last):
+        far = (o + step) % wide_z
+
+        def one(yp, carry):
+            if step != 0:
+                remote_piece(far, step, yp).wait_send()
+                return carry
+            _, mine = owner(far, step, yp)
+
+            @pl.when(jnp.logical_not(mine))
+            def _():
+                remote_piece(far, step, yp).wait_send()
+
+            return carry
+
+        lax.fori_loop(first, last, one, 0)
+
+    plan = piece_plan(geo)
 
     def arrive(o, k):
         z_copy(o, o, k, up).wait_recv()
 
-    def z_step(d):
-        def part(k, carry):
-            arrive(d, k)
-            forward_up(d, k)
-            arrive(wide_z - d, k)
-            forward_down(d, k)
-            return carry
-
-        lax.fori_loop(0, chunks, part, 0)
-        hand_out(d)
-        hand_out(wide_z - d)
-
-    def z_step_before_last(d):
+    def level(n):
+        last = n == len(plan) - 1
         for k in range(chunks):
-            arrive(d, k)
-            if k < chunks // 2:
-                forward_up(d, k)
-            arrive(wide_z - d, k)
-            if k >= chunks // 2:
-                forward_down(d, k)
-        hand_out(d)
-        hand_out(wide_z - d)
-
-    def z_step_last(d):
-        for k in range(chunks):
-            arrive(d, k)
-        hand_out(d)
+            arrive(STRIDE * n, k)
+            if not last:
+                forward_up(STRIDE * n, k)
+            arrive(wide_z - STRIDE * n, k)
+            if not last:
+                forward_down(wide_z - STRIDE * n, k)
+        for one in plan[n]:
+            hand_out(*one)
 
     low64 = lane_low(DB)
     low32 = lane_low(HALF)
@@ -335,8 +355,8 @@
         energy = quotient(cross, norm)
         rest = image - energy * first
         second = jnp.where(used, apply(rest, q), 0.0)
-        ibuf[b] = pack(image)
-        gbuf[b] = pack(second)
+        gbuf[my_t, b, :HALF] = pack(second)
+        gbuf[my_t, b, HALF:DB] = pack(image)
         values = (
             norm,
             cross,
@@ -351,7 +371,30 @@
         tile = jnp.zeros((8, LANES), jnp.float32)
         for k, value in enumerate(values):
             tile = jnp.where(sub == k, value, tile)
-        stat_ref[b] = tile
+        gbuf[my_t, b, DB:] = tile
+        for i in range(1, wide_x):
+            g_block(b, i - 1, dev(x_term(i), my_z, my_y)).start()
+        g_block(b, wide_x - 1, sibling).start()
+
+    def g_block(b, k, peer):
+        return pltpu.make_async_remote_copy(
+            src_ref=gbuf.at[my_t, b],
+            dst_ref=gbuf.at[my_t, b],
+            send_sem=g_send.at[b, k],
+            recv_sem=g_recv.at[my_t],
+            device_id=peer,
+            device_id_type=MESH,
+        )
+
+    def g_copy(t, k, peer):
+        return pltpu.make_async_remote_copy(
+            src_ref=gbuf.at[t],
+            dst_ref=gbuf.at[t],
+            send_sem=g_pass.at[k],
+            recv_sem=g_recv.at[t],
+            device_id=peer,
+            device_id_type=MESH,
+        )
 
     def unpack_left():
         def one(t, carry):
@@ -367,35 +410,25 @@
 
         lax.fori_loop(0, terms, one, 0)
 
-    early = min(3, half_z - 1)
-    hand_out(0)
+    for one in plan[0]:
+        hand_out(*one)
     for i in range(1, wide_x):
         t = x_term(i)
         l_copy(t, sibling, 0).wait_recv()
         l_copy(t, sibling, wide_x - 1 + i).start()
-    lax.fori_loop(1, early, lambda d, c: (z_step(d), c)[1], 0)
-    for i in range(wide_x):
-        l_copy(lax.rem(my_x + i, wide_x) * 2 + 1 - my_c, sibling, 0).wait_recv()
-    unpack_left()
-    wave_copy.wait()
-
-    def mixed(d, carry):
-        z_step(d)
-        work(d - early)
-        return carry
-
-    lax.fori_loop(early, half_z - 1, mixed, 0)
-    z_step_before_last(half_z - 1)
-    work(half_z - 1 - early)
-    z_step_last(half_z)
-
-    def rest_of_work(i, carry):
-        work(i)
-        return carry
-
-    lax.fori_loop(half_z - early, nblk, rest_of_work, 0)
-
-    stat = {name: stat_ref[:, k, :] for k, name in enumerate(NAMES)}
+    done = 0
+    for n in range(1, len(plan)):
+        level(n)
+        if n == 1:
+            for i in range(wide_x):
+                l_copy(lax.rem(my_x + i, wide_x) * 2 + 1 - my_c, sibling, 0).wait_recv()
+            unpack_left()
+            wave_copy.wait()
+        until = nblk if n == len(plan) - 1 else (1 if n == 1 else STRIDE * n)
+        lax.fori_loop(done, until, lambda i, c: (work(i), c)[1], 0)
+        done = until
+
+    stat = {name: gbuf[my_t, :, DB + k, :] for k, name in enumerate(NAMES)}
     mine = my_t * wide_y + my_y
     red_a[mine] = row_of(merge(stat, False))
 
@@ -420,11 +453,17 @@
         )
 
     lax.fori_loop(1, plane, lambda i, c: (a_copy(i).start(), c)[1], 0)
+    for i in range(1, wide_x):
+        t = x_term(i)
+        g_copy(t, i - 1, sibling).wait_recv()
+        g_copy(t, i - 1, sibling).start()
     pltpu.make_async_copy(
         red_a.at[pl.ds(0, plane - 1)], red_a.at[pl.ds(0, plane - 1)], a_recv
     ).wait()
     red_b[my_z] = row_of(merge(read_rows(red_a), False))
     lax.fori_loop(1, wide_z, lambda i, c: (b_copy(i).start(), c)[1], 0)
+    for i in range(wide_x):
+        g_copy(lax.rem(my_x + i, wide_x) * 2 + 1 - my_c, 0, sibling).wait_recv()
     pltpu.make_async_copy(
         red_b.at[pl.ds(0, wide_z - 1)], red_b.at[pl.ds(0, wide_z - 1)], b_recv
     ).wait()
@@ -444,36 +483,16 @@
     )
 
     center = final["e"]
-    for b in range(nblk):
-        shift = stat_ref[b, 7:8, :] - center
-        fbuf[my_t * nblk + b] = (gbuf[b] + shift * ibuf[b]) * scale
-
-    def f_copy(t, peer, k):
-        return pltpu.make_async_remote_copy(
-            src_ref=fbuf.at[pl.ds(t * nblk, nblk)],
-            dst_ref=fbuf.at[pl.ds(t * nblk, nblk)],
-            send_sem=f_send.at[k],
-            recv_sem=f_recv.at[t],
-            device_id=peer,
-            device_id_type=MESH,
-        )
-
-    for i in range(1, wide_x):
-        f_copy(my_t, dev(x_term(i), my_z, my_y), i - 1).start()
-    f_copy(my_t, sibling, wide_x - 1).start()
-    for i in range(1, wide_x):
-        t = x_term(i)
-        f_copy(t, sibling, 0).wait_recv()
-        f_copy(t, sibling, wide_x - 1 + i).start()
-    for i in range(wide_x):
-        f_copy(lax.rem(my_x + i, wide_x) * 2 + 1 - my_c, sibling, 0).wait_recv()
+
+    def block(at):
+        t, b = at // nblk, lax.rem(at, nblk)
+        shift = gbuf[t, b, DB + 7 : DB + 8, :] - center
+        return (gbuf[t, b, :HALF] + shift * gbuf[t, b, HALF:DB]) * scale
 
     def place(q, carry):
         for u in range(pairs // 2):
-            first_at = tab[slot_at + q * pairs + 2 * u]
-            second_at = tab[slot_at + q * pairs + 2 * u + 1]
-            first = fbuf[first_at]
-            second = fbuf[second_at]
+            first = block(tab[slot_at + q * pairs + 2 * u])
+            second = block(tab[slot_at + q * pairs + 2 * u + 1])
             out_ref[q, 0:HALF, u * LANES : (u + 1) * LANES] = jnp.where(
                 low32, first, swap(second)
             )
@@ -484,32 +503,44 @@
 
     lax.fori_loop(0, sec, place, 0)
 
-    def z_done(d, carry):
+    for n in range(len(plan) - 1):
         for k in range(chunks):
-            z_copy(0, d + 1, k, up).wait_send()
-            z_copy(0, wide_z - 1 - d, k, down).wait_send()
-        return carry
-
-    lax.fori_loop(0, half_z - 1, z_done, 0)
-    for k in range(chunks):
-        z_copy(0, half_z, k, up).wait_send()
-
-    def p_done(n, carry):
-        o, yp = n // wide_y, lax.rem(n, wide_y)
-        _, mine = owner(o, yp)
-
-        @pl.when(jnp.logical_not(mine))
-        def _():
-            remote_piece(o, yp).wait_send()
-
-        return carry
-
-    lax.fori_loop(0, wide_z * wide_y, p_done, 0)
+            z_copy(0, STRIDE * (n + 1), k, up).wait_send()
+            z_copy(0, wide_z - STRIDE * (n + 1), k, down).wait_send()
+    for pieces in plan:
+        for one in pieces:
+            sent(*one)
     for i in range(2 * wide_x - 1):
         l_copy(my_t, sibling, i).wait_send()
-        f_copy(my_t, sibling, i).wait_send()
+
+    def g_done(b, carry):
+        for k in range(wide_x):
+            g_block(b, k, sibling).wait_send()
+        return carry
+
+    lax.fori_loop(0, nblk, g_done, 0)
+    for i in range(wide_x - 1):
+        g_copy(my_t, i, sibling).wait_send()
     lax.fori_loop(1, plane, lambda i, c: (a_copy(i).wait_send(), c)[1], 0)
     lax.fori_loop(1, wide_z, lambda i, c: (b_copy(i).wait_send(), c)[1], 0)
+
+
+def piece_plan(geo):
+    _, wide_y, wide_z = geo
+    levels = wide_z // (2 * STRIDE)
+    plan = []
+    for n in range(levels):
+        o = STRIDE * n
+        pieces = []
+        for step in range(STRIDE):
+            pieces.append((o, step, 0, wide_y))
+            if o + step > 0:
+                pieces.append(((wide_z - o) % wide_z, -step, 0, wide_y))
+        plan.append(pieces)
+    top = STRIDE * (levels - 1)
+    plan[-1].append((top, STRIDE, 0, wide_y // 2))
+    plan[-1].append(((wide_z - top) % wide_z, -STRIDE, wide_y // 2, wide_y))
+    return plan
 
 
 def tables(geo, sec, pairs, pair_target):
@@ -520,12 +551,21 @@
     my_s = lax.axis_index("sectors")
     my_z, my_y = my_s // wide_y, my_s % wide_y
     cells = sec * pairs
-    plane = lax.dynamic_slice_in_dim(pair_target, my_z * wide_y * sec, wide_y * sec, 0)
-    plane = plane.reshape(wide_y, cells)
-    offsets = jnp.arange(wide_z, dtype=jnp.int32)
-    run = jnp.remainder(my_z - offsets, wide_z) * wide_y + my_y
-    hit = (plane // sec)[None, :, :] == run[:, None, None]
-    wanted = jnp.sum(jnp.where(hit, (plane % sec)[None, :, :], 0), axis=2).reshape(-1)
+    slot_of, step_of = {}, {}
+    for pieces in piece_plan(geo):
+        for o, step, first, last in pieces:
+            for yp in range(first, last):
+                slot_of[(o + step) % wide_z, yp] = o
+                step_of[(o + step) % wide_z, yp] = step
+    keys = [(far, yp) for far in range(wide_z) for yp in range(wide_y)]
+    slots = jnp.array([slot_of[key] for key in keys], jnp.int32)
+    steps = jnp.array([step_of[key] for key in keys], jnp.int32)
+    columns = jnp.array([yp for _, yp in keys], jnp.int32)
+    readers = jnp.remainder(my_z + steps, wide_z) * wide_y + columns
+    run = jnp.remainder(my_z - slots, wide_z) * wide_y + my_y
+    asked = jnp.take(pair_target.reshape(wide_z * wide_y, cells), readers, axis=0)
+    hit = asked // sec == run[:, None]
+    wanted = jnp.sum(jnp.where(hit, asked % sec, 0), axis=1)
     own = lax.dynamic_slice_in_dim(pair_target, my_s * sec, sec, 0).reshape(cells)
     own_run = own // sec
     offset = jnp.remainder(my_z - own_run // wide_y, wide_z)
@@ -570,12 +610,9 @@
             pltpu.VMEM((sec, terms * DB, LANES), bf16),
             pltpu.VMEM((LANES, terms * DB), bf16),
             pltpu.VMEM((LANES, terms * DB), bf16),
-            pltpu.VMEM((nblk, HALF, LANES), f32),
-            pltpu.VMEM((nblk, HALF, LANES), f32),
-            pltpu.VMEM((nblk, 8, LANES), f32),
+            pltpu.VMEM((terms, nblk, DB + 8, LANES), f32),
             pltpu.VMEM((plane, 1, LANES), f32),
             pltpu.VMEM((geo[2], 1, LANES), f32),
-            pltpu.VMEM((terms * nblk, HALF, LANES), f32),
             dma,
             dma((geo[2], chunks)),
             dma((geo[2], chunks)),
@@ -587,8 +624,11 @@
             dma,
             dma((geo[2],)),
             dma,
-            dma((2 * geo[0] - 1,)),
+            dma((nblk, geo[0])),
+            dma((geo[0],)),
             dma((terms,)),
+            pltpu.SemaphoreType.REGULAR,
+            pltpu.SemaphoreType.REGULAR,
         ],
         compiler_params=pltpu.CompilerParams(
             collective_id=0, has_side_effects=True, vmem_limit_bytes=32 * 1024 * 1024

time: 90.9 us -> 74.4 us (0.82)
  Pallas kernels: 83.8 us -> 67.1 us
    pallas_call x1, Pallas kernels: 83.8 us -> 67.1 us  [per_device(): pl.pallas_call(functools.partial(kernel, geo, cells), out_shape=(jax.Shap...]
    unnamed x12 -> x19, local copies, waits for them, and re-layouts: 4.91 us -> 4.76 us
where the time goes in v2:
time: 74.4 us; the launch traced here: 74.2 us
  Pallas kernels  67.1 us (90%)
  local copies, waits for them, and re-layouts  5.8 us (8%)
  between operations  0.77 us (1%)
    pallas_call x1, Pallas kernels, per_device(): pl.pallas_call(functools.partial(kernel, geo, cells), out_shape=(jax.Shap...  67.1 us
    unnamed x19, local copies, waits for them, and re-layouts  4.76 us

profile of v2, /device:TPU:1, one launch (start us, length us, event | category | flops | bytes accessed | tf_op | source)
XLA Modules:
  0.0 74.2 jit_solution(12868866373389988800)
XLA Ops:
  0.6 0.0 copy-start.4
  0.7 0.0 copy-start.5
  0.7 0.0 copy-start.6
  0.7 0.6 copy-done.5
  1.3 0.0 copy-done.6
  1.4 0.1 constant_dynamic-slice_fusion
  1.5 0.1 copy.15
  1.5 0.1 reshape.137
  1.6 0.6 copy-done.7
  2.2 0.2 fusion.6
  2.5 0.1 copy.14
  2.6 0.1 reshape.136
  2.7 0.0 copy-start.1
  2.7 0.0 copy-start.2
  2.8 0.6 gather_fusion
  3.3 0.2 fusion.2
  3.6 0.0 copy-start.3
  3.6 0.1 concatenate.3.tab
  3.6 0.1 copy-done.2
  3.7 0.6 copy-done.3
  4.3 1.2 %copy-done = f32[8,64,512]{2,1,0:T(8,128)S(1)} copy-done((f32[8,64,512]{2,1,0:T(8,128)S(1)}, f32[8,64,512]{2,1,0:T(8,128)}, u32[]{:S(2)}) %copy-start) | copy-done | bytes 1048600
  5.5 67.1 %shard_map.95 = (f32[8,64,512]{2,1,0:T(8,128)S(1)}, f32[2,2]{1,0:T(2,128)S(1)}) custom-call(s32[160]{0:T(256)S(1)} %concatenate.3.tab, s32[512]{0:T(512)S(1)} %copy-done.3, f32[8,64,512]{2,1,0:T(8,128)S(1)} %copy-done, f32[8,4096]{1,0:T(8,128)S(1)} %bitcast.2, f32[8,4096]{1,0:T(8,128)S(1)} %bitcast.3), custom_call_target="tpu_custom_call" | custom-call | tf_op jit(solution)/shard_map/pallas_call | solution.py:596
  72.6 1.0 %copy.18 = f32[8,64,512]{2,1,0:T(8,128)} copy(f32[8,64,512]{2,1,0:T(8,128)S(1)} %get-tuple-element.15) | data formatting | bytes 2097152
  73.6 0.6 copy.19
  (10 shorter events, 0.1 us)
Async XLA Ops:
  0.6 0.7 copy-start.4
  0.7 0.7 copy-start.5
  0.7 0.7 copy-start.6
  1.5 0.7 copy-start.7
  2.7 0.9 %copy-start.1 = (f32[1,8,4096]{2,1,0:T(8,128)S(1)}, f32[1,8,4096]{2,1,0:T(8,128)}, u32[]{:S(2)}) copy-start(f32[1,8,4096]{2,1,0:T(8,128)} %param.9) | copy-start | bytes 393220
  2.7 1.0 %copy-start.2 = (f32[1,8,4096]{2,1,0:T(8,128)S(1)}, f32[1,8,4096]{2,1,0:T(8,128)}, u32[]{:S(2)}) copy-start(f32[1,8,4096]{2,1,0:T(8,128)} %param.10) | copy-start | bytes 393220
  3.6 0.7 copy-start.3
  4.3 1.2 %copy-start = (f32[8,64,512]{2,1,0:T(8,128)S(1)}, f32[8,64,512]{2,1,0:T(8,128)}, u32[]{:S(2)}) copy-start(f32[8,64,512]{2,1,0:T(8,128)} %wave_hbm.1) | copy-start | bytes 3145732

commit v3 on v2

--- a/solution.py
+++ b/solution.py
@@ -86,15 +86,23 @@
 
 def kernel(
     geo,
-    cells,
-    tab,
-    dims,
     wave_hbm,
-    left_ref,
-    right_ref,
+    left_hbm,
+    right_hbm,
+    target_hbm,
+    dims_hbm,
     out_ref,
     proj_ref,
     wave,
+    left_ref,
+    right_ref,
+    target_ref,
+    dims,
+    asked,
+    tab_vmem,
+    tab,
+    other,
+    shifts,
     zbuf,
     stage,
     rrecv,
@@ -105,7 +113,8 @@
     gbuf,
     red_a,
     red_b,
-    wave_sem,
+    in_sem,
+    tab_sem,
     z_send,
     z_recv,
     p_send,
@@ -126,7 +135,8 @@
     terms = 2 * wide_x
     nblk = wide_z // 2
     half_z = wide_z // 2
-    sec = left_ref.shape[0]
+    sec, pairs = wave.shape[0], wave.shape[2] // DB
+    cells = sec * pairs
     chunks = z_send.shape[1]
     csec = sec // chunks
     plane = terms * wide_y
@@ -164,9 +174,23 @@
     z_near = [z_peer(i) for i in near]
     y_near = [y_peer(i) for i in range(1, wide_y)]
     tell(barrier, z_near + y_near + [term_peer(i) for i in range(1, terms)])
-    wave_copy = pltpu.make_async_copy(wave_hbm, wave, wave_sem)
-    wave_copy.start()
+    loads = [
+        pltpu.make_async_copy(src, dst, in_sem.at[k])
+        for k, (src, dst) in enumerate(
+            (
+                (right_hbm.at[0], right_ref),
+                (left_hbm.at[0], left_ref),
+                (target_hbm, target_ref),
+                (dims_hbm, dims),
+                (wave_hbm, wave),
+            )
+        )
+    ]
+    for load in loads:
+        load.start()
+    loads[0].wait()
     repack(right_ref, zbuf.at[0])
+    loads[1].wait()
     repack(left_ref, lall.at[my_t])
     pl.semaphore_wait(barrier, len(near) + wide_y - 1 + terms - 1)
 
@@ -214,6 +238,55 @@
     tell(plane_sem, y_near)
     pl.semaphore_wait(plane_sem, wide_y - 1)
     tell(space_sem, z_near)
+
+    plan = piece_plan(geo)
+    for k in range(2, 5):
+        loads[k].wait()
+    width = min(LANES, target_ref.shape[1])
+    sec_bits, y_bits = sec.bit_length() - 1, wide_y.bit_length() - 1
+    tile_lane = lax.broadcasted_iota(jnp.int32, (pairs, width), 1)
+    tile_row = lax.broadcasted_iota(jnp.int32, (pairs, width), 0)
+
+    def run_tile(run):
+        base = lax.div(run * sec, width) * width
+        tile = target_ref[:, pl.ds(pl.multiple_of(base, width), width)]
+        return tile, ((tile_lane + base) >> sec_bits) == run
+
+    def ask(o, step, first, last):
+        far = (o + step) % wide_z
+        wanted = lax.rem(my_z + (wide_z - o), wide_z) * wide_y + my_y
+
+        def one(yp, carry):
+            reader = lax.rem(my_z + (wide_z + step), wide_z) * wide_y + yp
+            tile, own = run_tile(reader)
+            hit = jnp.logical_and(own, (tile >> sec_bits) == wanted)
+            value = total(jnp.where(hit, (tile & (sec - 1)).astype(jnp.float32), 0.0))
+            asked[far, yp] = jnp.broadcast_to(value, (8, LANES))
+            return carry
+
+        lax.fori_loop(first, last, one, 0)
+
+    for pieces in plan:
+        for one in pieces:
+            ask(*one)
+    tile, own = run_tile(my_s)
+    run = tile >> sec_bits
+    far = (my_z - (run >> y_bits) + wide_z) & (wide_z - 1)
+    column = ((run & (wide_y - 1)) + my_y + far) & (wide_x - 1)
+    slot = (2 * column + (far >> (half_z.bit_length() - 1))) * nblk + (far & (nblk - 1))
+    tab_vmem[0:pairs, 0:width] = slot
+    full_row = lax.broadcasted_iota(jnp.int32, (8, LANES), 0)
+    full_lane = lax.broadcasted_iota(jnp.int32, (8, LANES), 1)
+    found = jnp.zeros((8, LANES), jnp.float32)
+    for b in range(nblk):
+        hit = jnp.logical_and(own, slot == my_t * nblk + b)
+        for k, what in enumerate((tile_lane & (sec - 1), tile_row, tile)):
+            value = total(jnp.where(hit, what.astype(jnp.float32), 0.0))
+            here = jnp.logical_and(full_row == b, full_lane == k)
+            found = jnp.where(here, value, found)
+    tab_vmem[8:16, :] = found.astype(jnp.int32)
+    tab_copy = pltpu.make_async_copy(tab_vmem, tab, tab_sem)
+    tab_copy.start()
     pl.semaphore_wait(space_sem, len(near))
 
     def owner(far, step, yp):
@@ -241,11 +314,13 @@
         far = (o + step) % wide_z
 
         def one(yp, carry):
-            wanted = jnp.full((HALF, LANES), tab[far * wide_y + yp], jnp.int32)
-            got = zbuf[o, 0]
-            for k in range(1, sec):
-                got = jnp.where(wanted == k, zbuf[o, k], got)
-            stage[far, yp] = got
+            wanted = asked[far, yp]
+            picks = [wanted == k for k in range(1, sec)]
+            for r in range(0, HALF, 8):
+                got = zbuf[o, 0, r : r + 8]
+                for k in range(1, sec):
+                    got = jnp.where(picks[k - 1], zbuf[o, k, r : r + 8], got)
+                stage[far, yp, r : r + 8] = got
             if step != 0:
                 remote_piece(far, step, yp).start()
                 return carry
@@ -279,8 +354,6 @@
             return carry
 
         lax.fori_loop(first, last, one, 0)
-
-    plan = piece_plan(geo)
 
     def arrive(o, k):
         z_copy(o, o, k, up).wait_recv()
@@ -299,88 +372,98 @@
 
     low64 = lane_low(DB)
     low32 = lane_low(HALF)
-    slot_at = wide_z * wide_y
-    sector_at = slot_at + cells
-    column_at = sector_at + nblk
-    odd_at = column_at + nblk
-    target_at = odd_at + nblk
-    pairs = cells // sec
-
-    def apply(vec, q):
-        vh, vl = split(vec)
-        rhs = jnp.concatenate([vh, vh, vl, vl], axis=0)
+    lane = lax.broadcasted_iota(jnp.int32, (DB, LANES), 1)
+    row = lax.broadcasted_iota(jnp.int32, (DB, LANES), 0)
+
+    both_now = range(2)
+
+    def apply(vecs, qs):
+        rhs = []
+        for k in both_now:
+            vh, vl = split(vecs[k])
+            rhs.append(jnp.concatenate([vh, vh, vl, vl], axis=0))
         for u in range(terms // 2):
-            lhs = lbf[q, pl.ds(u * LANES, LANES), :]
-            both = jnp.dot(
-                jnp.concatenate([lhs, lhs], axis=1), rhs, preferred_element_type=jnp.float32
+            for k in both_now:
+                lhs = lbf[qs[k], u * LANES : (u + 1) * LANES, :]
+                part = jnp.dot(
+                    jnp.concatenate([lhs, lhs], axis=1), rhs[k], preferred_element_type=jnp.float32
+                )
+                high, low = split(jnp.where(low64, part[:DB], part[DB:]))
+                wcat[k, :DB, u * LANES : (u + 1) * LANES] = high
+                wcat[k, DB:, u * LANES : (u + 1) * LANES] = low
+        outs = []
+        for k in both_now:
+            out = lax.dot_general(
+                wcat[k], rcat[k], (((1,), (1,)), ((), ())), preferred_element_type=jnp.float32
             )
-            high, low = split(jnp.where(low64, both[:DB], both[DB:]))
-            wcat[:DB, u * LANES : (u + 1) * LANES] = high
-            wcat[DB:, u * LANES : (u + 1) * LANES] = low
-        out = lax.dot_general(
-            wcat[...], rcat[...], (((1,), (1,)), ((), ())), preferred_element_type=jnp.float32
-        )
-        out = out[:DB] + out[DB:]
-        return out + swap(out)
+            out = out[:DB] + out[DB:]
+            outs.append(out + swap(out))
+        return outs
 
     def pack(x):
         return jnp.where(low32, x[:HALF], x[HALF:])
 
-    def work(i):
-        b = jnp.where(my_c == 0, i, nblk - 1 - i)
-        pltpu.make_async_copy(rrecv.at[b], rrecv.at[b], p_recv.at[b]).wait()
-        for u in range(terms // 2):
-            first, second = rrecv[b, 2 * u], rrecv[b, 2 * u + 1]
-            top = jnp.where(low32, first, swap(second))
-            bottom = jnp.where(low32, swap(first), second)
-            high, low = split(jnp.concatenate([top, bottom], axis=0))
-            rcat[:DB, u * LANES : (u + 1) * LANES] = high
-            rcat[DB:, u * LANES : (u + 1) * LANES] = low
-        q = tab[sector_at + b]
-        column = jnp.full((DB, LANES), tab[column_at + b], jnp.int32)
-        odd = jnp.full((DB, LANES), tab[odd_at + b], jnp.int32)
-        raw = wave[q, :, 0:LANES]
-        for u in range(1, pairs // 2):
-            raw = jnp.where(column == u, wave[q, :, u * LANES : (u + 1) * LANES], raw)
-        lane = lax.broadcasted_iota(jnp.int32, (DB, LANES), 1)
-        row = lax.broadcasted_iota(jnp.int32, (DB, LANES), 0)
-        raw = jnp.where(lane // DB == odd, raw, swap(raw))
-        used = jnp.logical_and(
-            row < dims[my_s * sec + q], lax.rem(lane, DB) < dims[tab[target_at + b]]
-        )
-        first = jnp.where(used, raw, 0.0)
-        image = jnp.where(used, apply(first, q), 0.0)
-        norm = 0.5 * total(first * first)
-        cross = 0.5 * total(first * image)
-        energy = quotient(cross, norm)
-        rest = image - energy * first
-        second = jnp.where(used, apply(rest, q), 0.0)
-        gbuf[my_t, b, :HALF] = pack(second)
-        gbuf[my_t, b, HALF:DB] = pack(image)
-        values = (
-            norm,
-            cross,
-            0.5 * total(rest * rest),
-            0.5 * total(rest * first),
-            0.5 * total(first * second),
-            0.5 * total(rest * image),
-            0.5 * total(rest * second),
-            energy,
-        )
+    def work(m):
+        low_b = jnp.where(my_c == 0, 2 * m, nblk - 2 - 2 * m)
+        bs = [low_b, low_b + 1]
+        for b in bs:
+            pltpu.make_async_copy(rrecv.at[b], rrecv.at[b], p_recv.at[b]).wait()
+        for k, b in enumerate(bs):
+            for u in range(terms // 2):
+                first, second = rrecv[b, 2 * u], rrecv[b, 2 * u + 1]
+                top = jnp.where(low32, first, swap(second))
+                bottom = jnp.where(low32, swap(first), second)
+                high, low = split(jnp.concatenate([top, bottom], axis=0))
+                rcat[k, :DB, u * LANES : (u + 1) * LANES] = high
+                rcat[k, DB:, u * LANES : (u + 1) * LANES] = low
+        qs, useds, firsts = [], [], []
+        for b in bs:
+            q, j = tab[8 + b, 0] & (sec - 1), tab[8 + b, 1]
+            target = tab[8 + b, 2] & (dims.shape[0] - 1)
+            column = jnp.full((DB, LANES), j >> 1, jnp.int32)
+            odd = jnp.full((DB, LANES), j & 1, jnp.int32)
+            raw = wave[q, :, 0:LANES]
+            for u in range(1, pairs // 2):
+                raw = jnp.where(column == u, wave[q, :, u * LANES : (u + 1) * LANES], raw)
+            raw = jnp.where((lane >> 6) == odd, raw, swap(raw))
+            used = jnp.logical_and(row < dims[my_s * sec + q], (lane & (DB - 1)) < dims[target])
+            qs.append(q)
+            useds.append(used)
+            firsts.append(jnp.where(used, raw, 0.0))
+        images = [jnp.where(useds[k], x, 0.0) for k, x in enumerate(apply(firsts, qs))]
+        norms = [0.5 * total(firsts[k] * firsts[k]) for k in both_now]
+        crosses = [0.5 * total(firsts[k] * images[k]) for k in both_now]
+        energies = [quotient(crosses[k], norms[k]) for k in both_now]
+        rests = [images[k] - energies[k] * firsts[k] for k in both_now]
+        seconds = [jnp.where(useds[k], x, 0.0) for k, x in enumerate(apply(rests, qs))]
         sub = lax.broadcasted_iota(jnp.int32, (8, LANES), 0)
-        tile = jnp.zeros((8, LANES), jnp.float32)
-        for k, value in enumerate(values):
-            tile = jnp.where(sub == k, value, tile)
-        gbuf[my_t, b, DB:] = tile
-        for i in range(1, wide_x):
-            g_block(b, i - 1, dev(x_term(i), my_z, my_y)).start()
-        g_block(b, wide_x - 1, sibling).start()
-
-    def g_block(b, k, peer):
+        for k, b in enumerate(bs):
+            first, image, rest, second = firsts[k], images[k], rests[k], seconds[k]
+            gbuf[my_t, b, :HALF] = pack(second)
+            gbuf[my_t, b, HALF:DB] = pack(image)
+            values = (
+                norms[k],
+                crosses[k],
+                0.5 * total(rest * rest),
+                0.5 * total(rest * first),
+                0.5 * total(first * second),
+                0.5 * total(rest * image),
+                0.5 * total(rest * second),
+                energies[k],
+            )
+            tile = jnp.zeros((8, LANES), jnp.float32)
+            for n, value in enumerate(values):
+                tile = jnp.where(sub == n, value, tile)
+            gbuf[my_t, b, DB:] = tile
+        for i in far_first(wide_x):
+            g_pair(low_b, i - 1, dev(x_term(i), my_z, my_y)).start()
+        g_pair(low_b, wide_x - 1, sibling).start()
+
+    def g_pair(b, k, peer):
         return pltpu.make_async_remote_copy(
-            src_ref=gbuf.at[my_t, b],
-            dst_ref=gbuf.at[my_t, b],
-            send_sem=g_send.at[b, k],
+            src_ref=gbuf.at[my_t, pl.ds(b, 2)],
+            dst_ref=gbuf.at[my_t, pl.ds(b, 2)],
+            send_sem=g_send.at[b // 2, k],
             recv_sem=g_recv.at[my_t],
             device_id=peer,
             device_id_type=MESH,
@@ -412,21 +495,22 @@
 
     for one in plan[0]:
         hand_out(*one)
-    for i in range(1, wide_x):
-        t = x_term(i)
-        l_copy(t, sibling, 0).wait_recv()
-        l_copy(t, sibling, wide_x - 1 + i).start()
-    done = 0
-    for n in range(1, len(plan)):
+    levels = len(plan) - 1
+    for n in range(1, levels + 1):
         level(n)
         if n == 1:
+            for i in range(1, wide_x):
+                t = x_term(i)
+                l_copy(t, sibling, 0).wait_recv()
+                l_copy(t, sibling, wide_x - 1 + i).start()
+            tab_copy.wait()
+        if n == min(2, levels):
             for i in range(wide_x):
                 l_copy(lax.rem(my_x + i, wide_x) * 2 + 1 - my_c, sibling, 0).wait_recv()
             unpack_left()
-            wave_copy.wait()
-        until = nblk if n == len(plan) - 1 else (1 if n == 1 else STRIDE * n)
-        lax.fori_loop(done, until, lambda i, c: (work(i), c)[1], 0)
-        done = until
+            if levels > 2:
+                lax.fori_loop(0, 2, lambda m, c: (work(m), c)[1], 0)
+    lax.fori_loop(2 if levels > 2 else 0, nblk // 2, lambda m, c: (work(m), c)[1], 0)
 
     stat = {name: gbuf[my_t, :, DB + k, :] for k, name in enumerate(NAMES)}
     mine = my_t * wide_y + my_y
@@ -461,9 +545,48 @@
         red_a.at[pl.ds(0, plane - 1)], red_a.at[pl.ds(0, plane - 1)], a_recv
     ).wait()
     red_b[my_z] = row_of(merge(read_rows(red_a), False))
-    lax.fori_loop(1, wide_z, lambda i, c: (b_copy(i).start(), c)[1], 0)
+    for i in far_first(wide_z):
+        b_copy(i).start()
     for i in range(wide_x):
         g_copy(lax.rem(my_x + i, wide_x) * 2 + 1 - my_c, 0, sibling).wait_recv()
+
+    def place(q, carry):
+        for u in range(pairs // 2):
+            ats = [tab[2 * u + k, lax.rem(my_s * sec, width) + q] for k in range(2)]
+            parts = [(at // nblk, lax.rem(at, nblk)) for at in ats]
+            for dst, lo in ((out_ref, 0), (other, HALF)):
+                first, second = [gbuf[t, b, lo : lo + HALF] for t, b in parts]
+                dst[q, 0:HALF, u * LANES : (u + 1) * LANES] = jnp.where(
+                    low32, first, swap(second)
+                )
+                dst[q, HALF:DB, u * LANES : (u + 1) * LANES] = jnp.where(
+                    low32, swap(first), second
+                )
+            first, second = [gbuf[t, b, DB : DB + 8] for t, b in parts]
+            shifts[q, :, u * LANES : (u + 1) * LANES] = jnp.where(low32[:8], first, second)
+        return carry
+
+    lax.fori_loop(0, sec, place, 0)
+
+    for n in range(len(plan) - 1):
+        for k in range(chunks):
+            z_copy(0, STRIDE * (n + 1), k, up).wait_send()
+            z_copy(0, wide_z - STRIDE * (n + 1), k, down).wait_send()
+    for pieces in plan:
+        for one in pieces:
+            sent(*one)
+    for i in range(2 * wide_x - 1):
+        l_copy(my_t, sibling, i).wait_send()
+
+    def g_done(b, carry):
+        for k in range(wide_x):
+            g_pair(2 * b, k, sibling).wait_send()
+        return carry
+
+    lax.fori_loop(0, nblk // 2, g_done, 0)
+    for i in range(wide_x - 1):
+        g_copy(my_t, i, sibling).wait_send()
+    lax.fori_loop(1, plane, lambda i, c: (a_copy(i).wait_send(), c)[1], 0)
     pltpu.make_async_copy(
         red_b.at[pl.ds(0, wide_z - 1)], red_b.at[pl.ds(0, wide_z - 1)], b_recv
     ).wait()
@@ -482,47 +605,18 @@
         / cell_total
     )
 
-    center = final["e"]
-
-    def block(at):
-        t, b = at // nblk, lax.rem(at, nblk)
-        shift = gbuf[t, b, DB + 7 : DB + 8, :] - center
-        return (gbuf[t, b, :HALF] + shift * gbuf[t, b, HALF:DB]) * scale
-
-    def place(q, carry):
-        for u in range(pairs // 2):
-            first = block(tab[slot_at + q * pairs + 2 * u])
-            second = block(tab[slot_at + q * pairs + 2 * u + 1])
-            out_ref[q, 0:HALF, u * LANES : (u + 1) * LANES] = jnp.where(
-                low32, first, swap(second)
-            )
-            out_ref[q, HALF:DB, u * LANES : (u + 1) * LANES] = jnp.where(
-                low32, swap(first), second
-            )
+    def finish(q, carry):
+        shift = shifts[q, 7:8, :] - final["e"]
+        out_ref[q] = (out_ref[q] + shift * other[q]) * scale
         return carry
 
-    lax.fori_loop(0, sec, place, 0)
-
-    for n in range(len(plan) - 1):
-        for k in range(chunks):
-            z_copy(0, STRIDE * (n + 1), k, up).wait_send()
-            z_copy(0, wide_z - STRIDE * (n + 1), k, down).wait_send()
-    for pieces in plan:
-        for one in pieces:
-            sent(*one)
-    for i in range(2 * wide_x - 1):
-        l_copy(my_t, sibling, i).wait_send()
-
-    def g_done(b, carry):
-        for k in range(wide_x):
-            g_block(b, k, sibling).wait_send()
-        return carry
-
-    lax.fori_loop(0, nblk, g_done, 0)
-    for i in range(wide_x - 1):
-        g_copy(my_t, i, sibling).wait_send()
-    lax.fori_loop(1, plane, lambda i, c: (a_copy(i).wait_send(), c)[1], 0)
+    lax.fori_loop(0, sec, finish, 0)
+
     lax.fori_loop(1, wide_z, lambda i, c: (b_copy(i).wait_send(), c)[1], 0)
+
+
+def far_first(count):
+    return sorted(range(1, count), key=lambda i: -min(i, count - i))
 
 
 def piece_plan(geo):
@@ -543,76 +637,48 @@
     return plan
 
 
-def tables(geo, sec, pairs, pair_target):
-    wide_x, wide_y, wide_z = geo
-    nblk = wide_z // 2
-    half_z = wide_z // 2
-    my_t = lax.axis_index("terms")
-    my_s = lax.axis_index("sectors")
-    my_z, my_y = my_s // wide_y, my_s % wide_y
-    cells = sec * pairs
-    slot_of, step_of = {}, {}
-    for pieces in piece_plan(geo):
-        for o, step, first, last in pieces:
-            for yp in range(first, last):
-                slot_of[(o + step) % wide_z, yp] = o
-                step_of[(o + step) % wide_z, yp] = step
-    keys = [(far, yp) for far in range(wide_z) for yp in range(wide_y)]
-    slots = jnp.array([slot_of[key] for key in keys], jnp.int32)
-    steps = jnp.array([step_of[key] for key in keys], jnp.int32)
-    columns = jnp.array([yp for _, yp in keys], jnp.int32)
-    readers = jnp.remainder(my_z + steps, wide_z) * wide_y + columns
-    run = jnp.remainder(my_z - slots, wide_z) * wide_y + my_y
-    asked = jnp.take(pair_target.reshape(wide_z * wide_y, cells), readers, axis=0)
-    hit = asked // sec == run[:, None]
-    wanted = jnp.sum(jnp.where(hit, asked % sec, 0), axis=1)
-    own = lax.dynamic_slice_in_dim(pair_target, my_s * sec, sec, 0).reshape(cells)
-    own_run = own // sec
-    offset = jnp.remainder(my_z - own_run // wide_y, wide_z)
-    holder = 2 * ((own_run % wide_y + my_y + offset) % wide_x) + offset // half_z
-    slot = holder * nblk + offset % half_z
-    chosen = slot[None, :] == (my_t * nblk + jnp.arange(nblk, dtype=jnp.int32))[:, None]
-    cell = jnp.sum(jnp.where(chosen, jnp.arange(cells, dtype=jnp.int32)[None, :], 0), axis=1)
-    target = jnp.sum(jnp.where(chosen, own[None, :], 0), axis=1)
-    column = cell % pairs
-    return jnp.concatenate([wanted, slot, cell // pairs, column // 2, column % 2, target])
-
-
 def per_device(wide_y, wave, left_env, right_env, pair_target, block_dims):
     terms = lax.axis_size("terms")
     devices = lax.axis_size("sectors")
     geo = (terms // 2, wide_y, devices // wide_y)
     sec = wave.shape[0]
     pairs = wave.shape[2] // DB
-    cells = sec * pairs
     nblk = geo[2] // 2
     plane = terms * wide_y
-    chunks = 2
-    tab = tables(geo, sec, pairs, pair_target)
+    chunks = 4
     f32, bf16 = jnp.float32, jnp.bfloat16
     dma = pltpu.SemaphoreType.DMA
     vmem = pl.BlockSpec(memory_space=pltpu.VMEM)
-    smem = pl.BlockSpec(memory_space=pltpu.SMEM)
     return pl.pallas_call(
-        functools.partial(kernel, geo, cells),
+        functools.partial(kernel, geo),
         out_shape=(
             jax.ShapeDtypeStruct(wave.shape, f32),
             jax.ShapeDtypeStruct((2, 2), f32),
         ),
-        in_specs=[smem, smem, pl.BlockSpec(memory_space=pl.ANY), vmem, vmem],
+        in_specs=[pl.BlockSpec(memory_space=pl.ANY)] * 5,
         out_specs=(vmem, vmem),
         scratch_shapes=[
             pltpu.VMEM(wave.shape, f32),
+            pltpu.VMEM((sec, DB * DB), f32),
+            pltpu.VMEM((sec, DB * DB), f32),
+            pltpu.VMEM((pairs, pair_target.shape[0]), jnp.int32),
+            pltpu.SMEM(block_dims.shape, jnp.int32),
+            pltpu.VMEM((geo[2], wide_y, 8, LANES), f32),
+            pltpu.VMEM((16, LANES), jnp.int32),
+            pltpu.SMEM((16, LANES), jnp.int32),
+            pltpu.VMEM(wave.shape, f32),
+            pltpu.VMEM((sec, 8, pairs * DB), f32),
             pltpu.VMEM((geo[2], sec, HALF, LANES), f32),
             pltpu.VMEM((geo[2], wide_y, HALF, LANES), f32),
             pltpu.VMEM((nblk, terms, HALF, LANES), f32),
             pltpu.VMEM((terms, sec, HALF, LANES), f32),
             pltpu.VMEM((sec, terms * DB, LANES), bf16),
-            pltpu.VMEM((LANES, terms * DB), bf16),
-            pltpu.VMEM((LANES, terms * DB), bf16),
+            pltpu.VMEM((2, LANES, terms * DB), bf16),
+            pltpu.VMEM((2, LANES, terms * DB), bf16),
             pltpu.VMEM((terms, nblk, DB + 8, LANES), f32),
             pltpu.VMEM((plane, 1, LANES), f32),
             pltpu.VMEM((geo[2], 1, LANES), f32),
+            dma((5,)),
             dma,
             dma((geo[2], chunks)),
             dma((geo[2], chunks)),
@@ -624,21 +690,21 @@
             dma,
             dma((geo[2],)),
             dma,
-            dma((nblk, geo[0])),
+            dma((nblk // 2, geo[0])),
             dma((geo[0],)),
             dma((terms,)),
             pltpu.SemaphoreType.REGULAR,
             pltpu.SemaphoreType.REGULAR,
         ],
         compiler_params=pltpu.CompilerParams(
-            collective_id=0, has_side_effects=True, vmem_limit_bytes=32 * 1024 * 1024
+            collective_id=0, has_side_effects=True, vmem_limit_bytes=56 * 1024 * 1024
         ),
     )(
-        tab,
+        wave,
+        left_env,
+        right_env,
+        pair_target.T,
         block_dims,
-        wave,
-        left_env.reshape(sec, DB * DB),
-        right_env.reshape(sec, DB * DB),
     )
 
 

time: 74.4 us -> 74.6 us (level)
  Pallas kernels: 67.1 us -> 71 us
  local copies, waits for them, and re-layouts: 5.8 us -> 2.83 us
    pallas_call x1, Pallas kernels: 67.1 us -> 71 us  [per_device(): pl.pallas_call(functools.partial(kernel, geo), out_shape=(jax.ShapeDtypeS...]
    unnamed x19 -> x4, local copies, waits for them, and re-layouts: 4.76 us -> 2.83 us
where the time goes in v3:
time: 74.6 us; the launch traced here: 74.4 us
  Pallas kernels  71 us (95%)
  local copies, waits for them, and re-layouts  2.83 us (4%)
    pallas_call x1, Pallas kernels, per_device(): pl.pallas_call(functools.partial(kernel, geo), out_shape=(jax.ShapeDtypeS...  71 us
    unnamed x4, local copies, waits for them, and re-layouts  2.83 us

profile of v3, /device:TPU:1, one launch (start us, length us, event | category | flops | bytes accessed | tf_op | source)
XLA Modules:
  0.0 74.4 jit_solution(10850790077795395696)
XLA Ops:
  0.6 71.0 %shard_map.68 = (f32[8,64,512]{2,1,0:T(8,128)}, f32[2,2]{1,0:T(2,128)}) custom-call(f32[8,64,512]{2,1,0:T(8,128)} %wave_hbm.1, f32[1,8,4096]{2,1,0:T(8,128)} %left_hbm.1, f32[1,8,4096]{2,1,0:T(8,128)} %right_hbm.1, s32[8,512]{1,0:T(8,128)} %bitcast.1, s32[512]{0:T(512)} %dims_hbm.1), custom_call_target="tpu_custom_call" | custom-call | tf_op jit(solution)/shard_map/pallas_call | solution.py:652
  71.6 0.0 copy-start
  71.6 2.3 %copy.9 = f32[8,64,512]{2,1,0:T(8,128)} copy(f32[8,64,512]{2,1,0:T(8,128)} %get-tuple-element.4) | data formatting | bytes 2097152
  73.9 0.0 copy-done
  73.9 0.6 copy.10
Async XLA Ops:
  71.6 2.3 %copy-start = (f32[2,2]{1,0:T(2,128)S(1)}, f32[2,2]{1,0:T(2,128)}, u32[]{:S(2)}) copy-start(f32[2,2]{1,0:T(2,128)} %get-tuple-element.5) | copy-start | bytes 52

commit v4 on v3

--- a/solution.py
+++ b/solution.py
@@ -91,7 +91,10 @@
     right_hbm,
     target_hbm,
     dims_hbm,
-    out_ref,
+    second_ref,
+    first_ref,
+    shift_ref,
+    sums_ref,
     proj_ref,
     wave,
     left_ref,
@@ -101,6 +104,7 @@
     asked,
     tab_vmem,
     tab,
+    ready,
     other,
     shifts,
     zbuf,
@@ -114,6 +118,7 @@
     red_a,
     red_b,
     in_sem,
+    out_sem,
     tab_sem,
     z_send,
     z_recv,
@@ -173,7 +178,6 @@
 
     z_near = [z_peer(i) for i in near]
     y_near = [y_peer(i) for i in range(1, wide_y)]
-    tell(barrier, z_near + y_near + [term_peer(i) for i in range(1, terms)])
     loads = [
         pltpu.make_async_copy(src, dst, in_sem.at[k])
         for k, (src, dst) in enumerate(
@@ -188,10 +192,9 @@
     ]
     for load in loads:
         load.start()
+    tell(barrier, z_near + y_near + [term_peer(i) for i in range(1, terms)])
     loads[0].wait()
     repack(right_ref, zbuf.at[0])
-    loads[1].wait()
-    repack(left_ref, lall.at[my_t])
     pl.semaphore_wait(barrier, len(near) + wide_y - 1 + terms - 1)
 
     def z_copy(src, dst, k, peer):
@@ -231,13 +234,13 @@
     for k in range(chunks):
         forward_up(0, k)
         forward_down(0, k)
+    loads[1].wait()
+    repack(left_ref, lall.at[my_t])
     for i in range(1, wide_x):
         l_copy(my_t, dev(x_term(i), my_z, my_y), i - 1).start()
     l_copy(my_t, sibling, wide_x - 1).start()
 
     tell(plane_sem, y_near)
-    pl.semaphore_wait(plane_sem, wide_y - 1)
-    tell(space_sem, z_near)
 
     plan = piece_plan(geo)
     for k in range(2, 5):
@@ -256,15 +259,15 @@
         far = (o + step) % wide_z
         wanted = lax.rem(my_z + (wide_z - o), wide_z) * wide_y + my_y
 
-        def one(yp, carry):
+        def one(yp):
             reader = lax.rem(my_z + (wide_z + step), wide_z) * wide_y + yp
             tile, own = run_tile(reader)
             hit = jnp.logical_and(own, (tile >> sec_bits) == wanted)
             value = total(jnp.where(hit, (tile & (sec - 1)).astype(jnp.float32), 0.0))
             asked[far, yp] = jnp.broadcast_to(value, (8, LANES))
-            return carry
-
-        lax.fori_loop(first, last, one, 0)
+
+        for yp in range(first, last):
+            one(yp)
 
     for pieces in plan:
         for one in pieces:
@@ -287,7 +290,8 @@
     tab_vmem[8:16, :] = found.astype(jnp.int32)
     tab_copy = pltpu.make_async_copy(tab_vmem, tab, tab_sem)
     tab_copy.start()
-    pl.semaphore_wait(space_sem, len(near))
+    pl.semaphore_wait(plane_sem, wide_y - 1)
+    tell(space_sem, z_near)
 
     def owner(far, step, yp):
         t = 2 * lax.rem(my_y + yp + far, wide_x) + far // half_z
@@ -358,16 +362,19 @@
     def arrive(o, k):
         z_copy(o, o, k, up).wait_recv()
 
-    def level(n):
-        last = n == len(plan) - 1
+    levels = len(plan) - 1
+
+    def relay(n):
         for k in range(chunks):
             arrive(STRIDE * n, k)
-            if not last:
+            if n < levels:
                 forward_up(STRIDE * n, k)
             arrive(wide_z - STRIDE * n, k)
-            if not last:
+            if n < levels:
                 forward_down(wide_z - STRIDE * n, k)
-        for one in plan[n]:
+
+    def pass_on(n):
+        for one in sorted(plan[n], key=lambda piece: -abs(piece[1])):
             hand_out(*one)
 
     low64 = lane_low(DB)
@@ -455,6 +462,9 @@
             for n, value in enumerate(values):
                 tile = jnp.where(sub == n, value, tile)
             gbuf[my_t, b, DB:] = tile
+        return low_b
+
+    def send_pair(low_b):
         for i in far_first(wide_x):
             g_pair(low_b, i - 1, dev(x_term(i), my_z, my_y)).start()
         g_pair(low_b, wide_x - 1, sibling).start()
@@ -493,11 +503,12 @@
 
         lax.fori_loop(0, terms, one, 0)
 
-    for one in plan[0]:
-        hand_out(*one)
-    levels = len(plan) - 1
     for n in range(1, levels + 1):
-        level(n)
+        relay(n)
+        if n == 1:
+            pl.semaphore_wait(space_sem, len(near))
+            pass_on(0)
+        pass_on(n)
         if n == 1:
             for i in range(1, wide_x):
                 t = x_term(i)
@@ -508,13 +519,14 @@
             for i in range(wide_x):
                 l_copy(lax.rem(my_x + i, wide_x) * 2 + 1 - my_c, sibling, 0).wait_recv()
             unpack_left()
-            if levels > 2:
-                lax.fori_loop(0, 2, lambda m, c: (work(m), c)[1], 0)
-    lax.fori_loop(2 if levels > 2 else 0, nblk // 2, lambda m, c: (work(m), c)[1], 0)
+            send_pair(work(0))
+    for m in range(1, nblk // 2 - 1):
+        send_pair(work(m))
+    last_pair = work(nblk // 2 - 1)
 
     stat = {name: gbuf[my_t, :, DB + k, :] for k, name in enumerate(NAMES)}
     mine = my_t * wide_y + my_y
-    red_a[mine] = row_of(merge(stat, False))
+    red_b[my_z] = row_of(merge(stat, False))
 
     def a_copy(i):
         return pltpu.make_async_remote_copy(
@@ -536,17 +548,18 @@
             device_id_type=MESH,
         )
 
+    for i in far_first(wide_z):
+        b_copy(i).start()
+    send_pair(last_pair)
+    pltpu.make_async_copy(
+        red_b.at[pl.ds(0, wide_z - 1)], red_b.at[pl.ds(0, wide_z - 1)], b_recv
+    ).wait()
+    red_a[mine] = row_of(merge(read_rows(red_b), False))
     lax.fori_loop(1, plane, lambda i, c: (a_copy(i).start(), c)[1], 0)
     for i in range(1, wide_x):
         t = x_term(i)
         g_copy(t, i - 1, sibling).wait_recv()
         g_copy(t, i - 1, sibling).start()
-    pltpu.make_async_copy(
-        red_a.at[pl.ds(0, plane - 1)], red_a.at[pl.ds(0, plane - 1)], a_recv
-    ).wait()
-    red_b[my_z] = row_of(merge(read_rows(red_a), False))
-    for i in far_first(wide_z):
-        b_copy(i).start()
     for i in range(wide_x):
         g_copy(lax.rem(my_x + i, wide_x) * 2 + 1 - my_c, 0, sibling).wait_recv()
 
@@ -554,7 +567,7 @@
         for u in range(pairs // 2):
             ats = [tab[2 * u + k, lax.rem(my_s * sec, width) + q] for k in range(2)]
             parts = [(at // nblk, lax.rem(at, nblk)) for at in ats]
-            for dst, lo in ((out_ref, 0), (other, HALF)):
+            for dst, lo in ((ready, 0), (other, HALF)):
                 first, second = [gbuf[t, b, lo : lo + HALF] for t, b in parts]
                 dst[q, 0:HALF, u * LANES : (u + 1) * LANES] = jnp.where(
                     low32, first, swap(second)
@@ -567,6 +580,12 @@
         return carry
 
     lax.fori_loop(0, sec, place, 0)
+    stores = [
+        pltpu.make_async_copy(src, dst, out_sem.at[k])
+        for k, (src, dst) in enumerate(((ready, second_ref), (other, first_ref), (shifts, shift_ref)))
+    ]
+    for store in stores:
+        store.start()
 
     for n in range(len(plan) - 1):
         for k in range(chunks):
@@ -586,11 +605,11 @@
     lax.fori_loop(0, nblk // 2, g_done, 0)
     for i in range(wide_x - 1):
         g_copy(my_t, i, sibling).wait_send()
-    lax.fori_loop(1, plane, lambda i, c: (a_copy(i).wait_send(), c)[1], 0)
+    lax.fori_loop(1, wide_z, lambda i, c: (b_copy(i).wait_send(), c)[1], 0)
     pltpu.make_async_copy(
-        red_b.at[pl.ds(0, wide_z - 1)], red_b.at[pl.ds(0, wide_z - 1)], b_recv
+        red_a.at[pl.ds(0, plane - 1)], red_a.at[pl.ds(0, plane - 1)], a_recv
     ).wait()
-    final = merge(read_rows(red_b), True)
+    final = merge(read_rows(red_a), True)
     cell_total = float(plane * wide_z * nblk * DB * DB)
     squared = jnp.maximum(final["rr"], 0.0)
     scale = 1.0 / jnp.sqrt(squared / cell_total + 1e-06)
@@ -605,14 +624,11 @@
         / cell_total
     )
 
-    def finish(q, carry):
-        shift = shifts[q, 7:8, :] - final["e"]
-        out_ref[q] = (out_ref[q] + shift * other[q]) * scale
-        return carry
-
-    lax.fori_loop(0, sec, finish, 0)
-
-    lax.fori_loop(1, wide_z, lambda i, c: (b_copy(i).wait_send(), c)[1], 0)
+    sub8 = lax.broadcasted_iota(jnp.int32, (8, LANES), 0)
+    sums_ref[...] = jnp.where(sub8 == 0, final["e"], scale)
+    for store in stores:
+        store.wait()
+    lax.fori_loop(1, plane, lambda i, c: (a_copy(i).wait_send(), c)[1], 0)
 
 
 def far_first(count):
@@ -649,14 +665,18 @@
     f32, bf16 = jnp.float32, jnp.bfloat16
     dma = pltpu.SemaphoreType.DMA
     vmem = pl.BlockSpec(memory_space=pltpu.VMEM)
-    return pl.pallas_call(
+    hbm = pl.BlockSpec(memory_space=pl.ANY)
+    second, first, shift, sums, projected = pl.pallas_call(
         functools.partial(kernel, geo),
         out_shape=(
             jax.ShapeDtypeStruct(wave.shape, f32),
+            jax.ShapeDtypeStruct(wave.shape, f32),
+            jax.ShapeDtypeStruct((sec, 8, pairs * DB), f32),
+            jax.ShapeDtypeStruct((8, LANES), f32),
             jax.ShapeDtypeStruct((2, 2), f32),
         ),
-        in_specs=[pl.BlockSpec(memory_space=pl.ANY)] * 5,
-        out_specs=(vmem, vmem),
+        in_specs=[hbm] * 5,
+        out_specs=(hbm, hbm, hbm, vmem, vmem),
         scratch_shapes=[
             pltpu.VMEM(wave.shape, f32),
             pltpu.VMEM((sec, DB * DB), f32),
@@ -666,6 +686,7 @@
             pltpu.VMEM((geo[2], wide_y, 8, LANES), f32),
             pltpu.VMEM((16, LANES), jnp.int32),
             pltpu.SMEM((16, LANES), jnp.int32),
+            pltpu.VMEM(wave.shape, f32),
             pltpu.VMEM(wave.shape, f32),
             pltpu.VMEM((sec, 8, pairs * DB), f32),
             pltpu.VMEM((geo[2], sec, HALF, LANES), f32),
@@ -679,6 +700,7 @@
             pltpu.VMEM((plane, 1, LANES), f32),
             pltpu.VMEM((geo[2], 1, LANES), f32),
             dma((5,)),
+            dma((3,)),
             dma,
             dma((geo[2], chunks)),
             dma((geo[2], chunks)),
@@ -706,6 +728,8 @@
         pair_target.T,
         block_dims,
     )
+    image_two = (second + (shift[:, 7:8, :] - sums[0, 0]) * first) * sums[1, 0]
+    return image_two, projected
 
 
 def solution(mesh, wide_y=WIDE_Y):

time: 74.6 us -> 71.3 us (0.956)
  Pallas kernels: 71 us -> 63.6 us
  other arithmetic: 0 us -> 4.88 us
  local copies, waits for them, and re-layouts: 2.83 us -> 1.83 us
    pallas_call x1, Pallas kernels: 71 us -> 63.6 us  [per_device(): pl.pallas_call(functools.partial(kernel, geo), out_shape=(jax.ShapeDtypeS...]
    mul x0 -> x1, other arithmetic: none -> 3.31 us  [per_device(): image_two = (second + (shift[:, 7:8, :] - sums[0, 0]) * first) * sums[1, 0]]
    unnamed x4, local copies, waits for them, and re-layouts: 2.83 us -> 0.57 us
    sub x0 -> x1, other arithmetic: none -> 1.57 us  [per_device(): image_two = (second + (shift[:, 7:8, :] - sums[0, 0]) * first) * sums[1, 0]]
    slice x0 -> x1, local copies, waits for them, and re-layouts: none -> 1.26 us  [per_device(): image_two = (second + (shift[:, 7:8, :] - sums[0, 0]) * first) * sums[1, 0]]
where the time goes in v4:
time: 71.3 us; the launch traced here: 71 us
  Pallas kernels  63.6 us (89%)
  other arithmetic  4.88 us (7%)
  local copies, waits for them, and re-layouts  1.83 us (3%)
    pallas_call x1, Pallas kernels, per_device(): pl.pallas_call(functools.partial(kernel, geo), out_shape=(jax.ShapeDtypeS...  63.6 us
    mul x1, other arithmetic, per_device(): image_two = (second + (shift[:, 7:8, :] - sums[0, 0]) * first) * sums[1, 0]  3.31 us
    sub x1, other arithmetic, per_device(): image_two = (second + (shift[:, 7:8, :] - sums[0, 0]) * first) * sums[1, 0]  1.57 us

profile of v4, /device:TPU:1, one launch (start us, length us, event | category | flops | bytes accessed | tf_op | source)
XLA Modules:
  0.0 71.0 jit_solution(18072382439211677445)
XLA Ops:
  0.6 63.6 %shard_map.68 = (f32[8,64,512]{2,1,0:T(8,128)}, f32[8,64,512]{2,1,0:T(8,128)}, f32[8,8,512]{2,1,0:T(8,128)}, f32[8,128]{1,0:T(8,128)}, f32[2,2]{1,0:T(2,128)}) custom-call(f32[8,64,512]{2,1,0:T(8,128)} %wave_hbm.1, f32[1,8,4096]{2,1,0:T(8,128)} %left_hbm.1, f32[1,8,4096]{2,1,0:T(8,128)} %right_hbm.1, s32[8,512]{1,0:T(8,128)} %bitcast.7, s32[512]{0:T(512)} %dims_hbm.1), custom_call_target="tpu_custom_call" | custom-call | tf_op jit(solution)/shard_map/pallas_call | solution.py:669
  64.3 1.3 %fusion = (f32[1,1]{1,0:T(1,128)}, f32[1,1]{1,0:T(1,128)}) fusion(f32[8,128]{1,0:T(8,128)} %get-tuple-element.9), kind=kLoop, calls=%fused_computation.3 | loop fusion | bytes 16 | tf_op jit(solution)/shard_map/slice | solution.py:731
  65.6 1.6 %slice_subtract_fusion = f32[8,1,512]{2,1,0:T(1,128)S(1)} fusion(f32[8,8,512]{2,1,0:T(8,128)} %get-tuple-element.8, f32[]{:T(128)} %bitcast.1), kind=kLoop, calls=%fused_computation.2 | loop fusion | flops 4096 | bytes 32772 | tf_op jit(solution)/shard_map/sub | solution.py:731
  67.1 0.0 copy-start
  67.1 3.3 %add_multiply_fusion = f32[8,64,512]{2,1,0:T(8,128)} fusion(f32[8,64,512]{2,1,0:T(8,128)} %get-tuple-element.7, f32[8,64,512]{2,1,0:T(8,128)} %get-tuple-element.10, f32[]{:T(128)} %bitcast.2, f32[8,512]{1,0:T(8,128)S(1)} %bitcast.6), kind=kLoop, calls=%fused_computation | loop fusion | flops 786432 | bytes 3162116 | tf_op jit(solution)/shard_map/mul | solution.py:731
  70.5 0.0 copy-done
  70.5 0.6 copy.11
  (1 shorter events, 0.0 us)
Async XLA Ops:
  67.1 3.3 %copy-start = (f32[2,2]{1,0:T(2,128)S(1)}, f32[2,2]{1,0:T(2,128)}, u32[]{:S(2)}) copy-start(f32[2,2]{1,0:T(2,128)} %get-tuple-element.17) | copy-start | bytes 52

commit v5 on v4

--- a/solution.py
+++ b/solution.py
@@ -91,10 +91,7 @@
     right_hbm,
     target_hbm,
     dims_hbm,
-    second_ref,
-    first_ref,
-    shift_ref,
-    sums_ref,
+    out_ref,
     proj_ref,
     wave,
     left_ref,
@@ -474,20 +471,26 @@
             src_ref=gbuf.at[my_t, pl.ds(b, 2)],
             dst_ref=gbuf.at[my_t, pl.ds(b, 2)],
             send_sem=g_send.at[b // 2, k],
-            recv_sem=g_recv.at[my_t],
+            recv_sem=g_recv.at[my_t, b // 2],
             device_id=peer,
             device_id_type=MESH,
         )
 
-    def g_copy(t, k, peer):
+    def g_copy(t, b, k, peer):
         return pltpu.make_async_remote_copy(
-            src_ref=gbuf.at[t],
-            dst_ref=gbuf.at[t],
-            send_sem=g_pass.at[k],
-            recv_sem=g_recv.at[t],
+            src_ref=gbuf.at[t, pl.ds(b, 2)],
+            dst_ref=gbuf.at[t, pl.ds(b, 2)],
+            send_sem=g_pass.at[b // 2, k],
+            recv_sem=g_recv.at[t, b // 2],
             device_id=peer,
             device_id_type=MESH,
         )
+
+    def pass_pair(m):
+        low_b = jnp.where(my_c == 0, 2 * m, nblk - 2 - 2 * m)
+        for i in range(1, wide_x):
+            g_copy(x_term(i), low_b, i - 1, sibling).wait_recv()
+            g_copy(x_term(i), low_b, i - 1, sibling).start()
 
     def unpack_left():
         def one(t, carry):
@@ -509,18 +512,16 @@
             pl.semaphore_wait(space_sem, len(near))
             pass_on(0)
         pass_on(n)
-        if n == 1:
+        if n == min(2, levels):
             for i in range(1, wide_x):
                 t = x_term(i)
                 l_copy(t, sibling, 0).wait_recv()
                 l_copy(t, sibling, wide_x - 1 + i).start()
-            tab_copy.wait()
-        if n == min(2, levels):
-            for i in range(wide_x):
-                l_copy(lax.rem(my_x + i, wide_x) * 2 + 1 - my_c, sibling, 0).wait_recv()
-            unpack_left()
-            send_pair(work(0))
-    for m in range(1, nblk // 2 - 1):
+    tab_copy.wait()
+    for i in range(wide_x):
+        l_copy(lax.rem(my_x + i, wide_x) * 2 + 1 - my_c, sibling, 0).wait_recv()
+    unpack_left()
+    for m in range(nblk // 2 - 1):
         send_pair(work(m))
     last_pair = work(nblk // 2 - 1)
 
@@ -551,17 +552,17 @@
     for i in far_first(wide_z):
         b_copy(i).start()
     send_pair(last_pair)
+    for m in range(nblk // 2 - 1):
+        pass_pair(m)
     pltpu.make_async_copy(
         red_b.at[pl.ds(0, wide_z - 1)], red_b.at[pl.ds(0, wide_z - 1)], b_recv
     ).wait()
     red_a[mine] = row_of(merge(read_rows(red_b), False))
     lax.fori_loop(1, plane, lambda i, c: (a_copy(i).start(), c)[1], 0)
-    for i in range(1, wide_x):
-        t = x_term(i)
-        g_copy(t, i - 1, sibling).wait_recv()
-        g_copy(t, i - 1, sibling).start()
-    for i in range(wide_x):
-        g_copy(lax.rem(my_x + i, wide_x) * 2 + 1 - my_c, 0, sibling).wait_recv()
+    pass_pair(nblk // 2 - 1)
+    for m in range(nblk // 2):
+        for i in range(wide_x):
+            g_copy(lax.rem(my_x + i, wide_x) * 2 + 1 - my_c, 2 * m, 0, sibling).wait_recv()
 
     def place(q, carry):
         for u in range(pairs // 2):
@@ -580,12 +581,6 @@
         return carry
 
     lax.fori_loop(0, sec, place, 0)
-    stores = [
-        pltpu.make_async_copy(src, dst, out_sem.at[k])
-        for k, (src, dst) in enumerate(((ready, second_ref), (other, first_ref), (shifts, shift_ref)))
-    ]
-    for store in stores:
-        store.start()
 
     for n in range(len(plan) - 1):
         for k in range(chunks):
@@ -603,8 +598,9 @@
         return carry
 
     lax.fori_loop(0, nblk // 2, g_done, 0)
-    for i in range(wide_x - 1):
-        g_copy(my_t, i, sibling).wait_send()
+    for m in range(nblk // 2):
+        for i in range(wide_x - 1):
+            g_copy(my_t, 2 * m, i, sibling).wait_send()
     lax.fori_loop(1, wide_z, lambda i, c: (b_copy(i).wait_send(), c)[1], 0)
     pltpu.make_async_copy(
         red_a.at[pl.ds(0, plane - 1)], red_a.at[pl.ds(0, plane - 1)], a_recv
@@ -624,11 +620,13 @@
         / cell_total
     )
 
-    sub8 = lax.broadcasted_iota(jnp.int32, (8, LANES), 0)
-    sums_ref[...] = jnp.where(sub8 == 0, final["e"], scale)
-    for store in stores:
-        store.wait()
+    for q in range(sec):
+        shift = shifts[q, 7:8, :] - final["e"][:, :1]
+        ready[q] = (ready[q] + shift * other[q]) * scale
+        pltpu.make_async_copy(ready.at[q], out_ref.at[q], out_sem.at[q]).start()
     lax.fori_loop(1, plane, lambda i, c: (a_copy(i).wait_send(), c)[1], 0)
+    for q in range(sec):
+        pltpu.make_async_copy(ready.at[q], out_ref.at[q], out_sem.at[q]).wait()
 
 
 def far_first(count):
@@ -666,17 +664,14 @@
     dma = pltpu.SemaphoreType.DMA
     vmem = pl.BlockSpec(memory_space=pltpu.VMEM)
     hbm = pl.BlockSpec(memory_space=pl.ANY)
-    second, first, shift, sums, projected = pl.pallas_call(
+    return pl.pallas_call(
         functools.partial(kernel, geo),
         out_shape=(
             jax.ShapeDtypeStruct(wave.shape, f32),
-            jax.ShapeDtypeStruct(wave.shape, f32),
-            jax.ShapeDtypeStruct((sec, 8, pairs * DB), f32),
-            jax.ShapeDtypeStruct((8, LANES), f32),
             jax.ShapeDtypeStruct((2, 2), f32),
         ),
         in_specs=[hbm] * 5,
-        out_specs=(hbm, hbm, hbm, vmem, vmem),
+        out_specs=(hbm, vmem),
         scratch_shapes=[
             pltpu.VMEM(wave.shape, f32),
             pltpu.VMEM((sec, DB * DB), f32),
@@ -700,7 +695,7 @@
             pltpu.VMEM((plane, 1, LANES), f32),
             pltpu.VMEM((geo[2], 1, LANES), f32),
             dma((5,)),
-            dma((3,)),
+            dma((sec,)),
             dma,
             dma((geo[2], chunks)),
             dma((geo[2], chunks)),
@@ -713,8 +708,8 @@
             dma((geo[2],)),
             dma,
             dma((nblk // 2, geo[0])),
-            dma((geo[0],)),
-            dma((terms,)),
+            dma((nblk // 2, geo[0])),
+            dma((terms, nblk // 2)),
             pltpu.SemaphoreType.REGULAR,
             pltpu.SemaphoreType.REGULAR,
         ],
@@ -728,8 +723,6 @@
         pair_target.T,
         block_dims,
     )
-    image_two = (second + (shift[:, 7:8, :] - sums[0, 0]) * first) * sums[1, 0]
-    return image_two, projected
 
 
 def solution(mesh, wide_y=WIDE_Y):

time: 71.3 us -> 66.3 us (0.930)
  other arithmetic: 4.88 us -> 0 us
  local copies, waits for them, and re-layouts: 1.83 us -> 2.83 us
  Pallas kernels: 63.6 us -> 62.7 us
    mul x1 -> x0, other arithmetic: 3.31 us -> none  [per_device(): image_two = (second + (shift[:, 7:8, :] - sums[0, 0]) * first) * sums[1, 0]]
    unnamed x4, local copies, waits for them, and re-layouts: 0.57 us -> 2.83 us
    sub x1 -> x0, other arithmetic: 1.57 us -> none  [per_device(): image_two = (second + (shift[:, 7:8, :] - sums[0, 0]) * first) * sums[1, 0]]
    slice x1 -> x0, local copies, waits for them, and re-layouts: 1.26 us -> none  [per_device(): image_two = (second + (shift[:, 7:8, :] - sums[0, 0]) * first) * sums[1, 0]]
    pallas_call x1, Pallas kernels: 63.6 us -> 62.7 us  [per_device(): pl.pallas_call(functools.partial(kernel, geo), out_shape=(jax.ShapeDtypeS...]
where the time goes in v5:
time: 66.3 us; the launch traced here: 66.1 us
  Pallas kernels  62.7 us (95%)
  local copies, waits for them, and re-layouts  2.83 us (4%)
    pallas_call x1, Pallas kernels, per_device(): pl.pallas_call(functools.partial(kernel, geo), out_shape=(jax.ShapeDtypeS...  62.7 us
    unnamed x4, local copies, waits for them, and re-layouts  2.83 us

profile of v5, /device:TPU:1, one launch (start us, length us, event | category | flops | bytes accessed | tf_op | source)
XLA Modules:
  0.0 66.1 jit_solution(13157128757998784382)
XLA Ops:
  0.6 62.7 %shard_map.68 = (f32[8,64,512]{2,1,0:T(8,128)}, f32[2,2]{1,0:T(2,128)}) custom-call(f32[8,64,512]{2,1,0:T(8,128)} %wave_hbm.1, f32[1,8,4096]{2,1,0:T(8,128)} %left_hbm.1, f32[1,8,4096]{2,1,0:T(8,128)} %right_hbm.1, s32[8,512]{1,0:T(8,128)} %bitcast.1, s32[512]{0:T(512)} %dims_hbm.1), custom_call_target="tpu_custom_call" | custom-call | tf_op jit(solution)/shard_map/pallas_call | solution.py:667
  63.3 0.0 copy-start
  63.3 2.3 %copy.9 = f32[8,64,512]{2,1,0:T(8,128)} copy(f32[8,64,512]{2,1,0:T(8,128)} %get-tuple-element.4) | data formatting | bytes 2097152
  65.6 0.0 copy-done
  65.6 0.6 copy.10
Async XLA Ops:
  63.3 2.3 %copy-start = (f32[2,2]{1,0:T(2,128)S(1)}, f32[2,2]{1,0:T(2,128)}, u32[]{:S(2)}) copy-start(f32[2,2]{1,0:T(2,128)} %get-tuple-element.5) | copy-start | bytes 52

commit v6 on v5

--- a/solution.py
+++ b/solution.py
@@ -337,7 +337,7 @@
 
             return carry
 
-        lax.fori_loop(first, last, one, 0)
+        lax.fori_loop(first, last, one, 0, unroll=True)
 
     def sent(o, step, first, last):
         far = (o + step) % wide_z

time: 66.3 us -> 66.2 us (level)
  no operation moved by 1% of the time
where the time goes in v6:
time: 66.2 us; the launch traced here: 66 us
  Pallas kernels  62.6 us (95%)
  local copies, waits for them, and re-layouts  2.83 us (4%)
    pallas_call x1, Pallas kernels, per_device(): pl.pallas_call(functools.partial(kernel, geo), out_shape=(jax.ShapeDtypeS...  62.6 us
    unnamed x4, local copies, waits for them, and re-layouts  2.83 us

profile of v6, /device:TPU:1, one launch (start us, length us, event | category | flops | bytes accessed | tf_op | source)
XLA Modules:
  0.0 66.0 jit_solution(11195296093746323847)
XLA Ops:
  0.6 62.6 %shard_map.68 = (f32[8,64,512]{2,1,0:T(8,128)}, f32[2,2]{1,0:T(2,128)}) custom-call(f32[8,64,512]{2,1,0:T(8,128)} %wave_hbm.1, f32[1,8,4096]{2,1,0:T(8,128)} %left_hbm.1, f32[1,8,4096]{2,1,0:T(8,128)} %right_hbm.1, s32[8,512]{1,0:T(8,128)} %bitcast.1, s32[512]{0:T(512)} %dims_hbm.1), custom_call_target="tpu_custom_call" | custom-call | tf_op jit(solution)/shard_map/pallas_call | solution.py:667
  63.2 0.0 copy-start
  63.2 2.3 %copy.9 = f32[8,64,512]{2,1,0:T(8,128)} copy(f32[8,64,512]{2,1,0:T(8,128)} %get-tuple-element.4) | data formatting | bytes 2097152
  65.5 0.0 copy-done
  65.5 0.6 copy.10
Async XLA Ops:
  63.2 2.3 %copy-start = (f32[2,2]{1,0:T(2,128)S(1)}, f32[2,2]{1,0:T(2,128)}, u32[]{:S(2)}) copy-start(f32[2,2]{1,0:T(2,128)} %get-tuple-element.5) | copy-start | bytes 52
